TPU v7x, 256 devices: a whole 4x4x8 slice. The times are simulated.
256 devices in a mesh: grp: 2 (over x_lo), gx: 32 (over x_hi, z, core), gy: 4 (over y).
Axes of the slice: x: 4 (x_hi: 2, x_lo: 2; x = x_hi * 2 + x_lo), y: 4, z: 8, core: 2. Of those that a mesh axis runs over, the one named last changes fastest.
Arguments:
- source: float32 [2, 512, 32, 256], P('grp', 'gx', 'gy'), may hold values from -8 to 8
- storage: float32 [2, 512, 32, 256], P('grp', 'gx', 'gy'), may hold values from 0.1 to 4
- host_device: int32 [16384, 1], P(('gx', 'gy')), may hold values from 0 to 127; in each aligned block of 128 rows (0 to 127, 128 to 255, ...) at most 2 rows name the same one
- host_column: int32 [16384], P(('gx', 'gy')), may hold values from 0 to 127
- inter_device: int32 [16384, 2], P(('gx', 'gy')), may hold values from 0 to 127, all different within a row; in each aligned block of 128 rows (0 to 127, 128 to 255, ...) at most 4 rows name the same one
- inter_slot: int32 [16384, 2], P(('gx', 'gy')), may hold values from 0 to 127
Outputs:
- pressure: float32 [2, 512, 32, 256], P('grp', 'gx', 'gy')
Inputs may be any that keep to these rules, and one draw needn't show every extreme that they name: `host_device`: in the rows of one device (128 aligned rows) no matrix device is named more than 2 times; some device is named exactly 2 times. `inter_device`: in the rows of one device no device is named more than 4 times; some device is named exactly 4 times; a row names distinct devices.
All inputs are finite; a program needn't handle non-finite values.
Results may differ from a plain program's by a relative error of at most 0.0001.
Values sent between devices are 32-bit elements; how exact they have to be, the bound alone decides.
A program may use at most 128 MiB of HBM per device.

v0:
```python
import jax
import jax.numpy as jnp
from jax import lax
from jax.sharding import PartitionSpec as P

TS = 16
INTERS = 2
SWEEPS = 2
DEGREE = 3
TILE = 256


TF = 2.0
TI = 1.0
TM = 0.5
LMIN = 0.3
LMAX = 3.0
HIGH = lax.Precision.HIGHEST


def with_halo(cells, sides, width):
    for axis, dim in sides:
        count = lax.axis_size(axis)
        ends = count - 1
        head = lax.slice_in_dim(cells, 0, width, axis=dim)
        tail = lax.slice_in_dim(cells, cells.shape[dim] - width, cells.shape[dim], axis=dim)
        cells = jnp.concatenate(
            [
                lax.ppermute(tail, axis, [(i, (i + 1) % count) for i in range(ends)]),
                cells,
                lax.ppermute(head, axis, [((i + 1) % count, i) for i in range(ends)]),
            ],
            axis=dim,
        )
    return cells


def swapped(value, axis, bit):
    return lax.ppermute(value, axis, [(i, i ^ 1 << bit) for i in range(lax.axis_size(axis))])


def in_plane(tiles):
    column = jnp.arange(TILE) % TS
    zero_col = jnp.zeros_like(tiles[:, :1])
    zero_row = jnp.zeros_like(tiles[:, :TS])
    left = jnp.where(column != 0, jnp.concatenate([zero_col, tiles[:, :-1]], 1), 0.0)
    right = jnp.where(column != TS - 1, jnp.concatenate([tiles[:, 1:], zero_col], 1), 0.0)
    upper = jnp.concatenate([zero_row, tiles[:, :-TS]], 1)
    lower = jnp.concatenate([tiles[:, TS:], zero_row], 1)
    return TF * (4.0 * tiles - left - right - upper - lower)


def slot_sources(dest, count, capacity, devices):
    onehot = (dest[:, None] == jnp.arange(devices, dtype=jnp.int32)[None, :]).astype(jnp.int32)
    earlier = jnp.cumsum(onehot, 0) - onehot
    rank = jnp.sum(onehot * earlier, 1)
    where_to = dest * capacity + rank
    empty = jnp.full((devices * capacity,), -1, jnp.int32)
    return empty.at[where_to].set(jnp.arange(count, dtype=jnp.int32))


def scatter_rows(labels, values, blocks):
    select = (labels[None, :] == jnp.arange(blocks, dtype=jnp.int32)[:, None]).astype(jnp.float32)
    return jnp.dot(select, values, precision=HIGH, preferred_element_type=jnp.float32)


def matrix_side(tiles_in, cols_in, columns):
    width = columns.shape[1]
    flat_tiles = tiles_in.reshape(-1, width)
    flat_cols = cols_in.reshape(-1)
    valid = flat_cols >= 0
    flux = jnp.where(valid[:, None], TM * (columns[jnp.maximum(flat_cols, 0)] - flat_tiles), 0.0)
    added = scatter_rows(flat_cols, flux, columns.shape[0])
    return (flux.reshape(tiles_in.shape), added)


def per_device(source, storage, host_device, host_column, inter_device, inter_slot):
    devices = lax.axis_size("gx") * lax.axis_size("gy")
    blocks = host_column.shape[0]
    width = source.shape[3]
    bx_cells = source.shape[1]
    by_cells = source.shape[2]
    cap_host = 2 * max(1, blocks // devices)
    cap_inter = 2 * max(2, blocks * INTERS // devices)
    is_frac = lax.axis_index("grp") == 1
    stored = storage[0]
    diag = jnp.where(is_frac, stored + 4.0 * TF + 2.0 * INTERS * TI + TM, stored + 6.0 + TM)
    host_src = slot_sources(host_device[:, 0], blocks, cap_host, devices)
    host_valid = host_src >= 0
    host_rows = jnp.maximum(host_src, 0)
    host_cols = jnp.where(host_valid, host_column[host_rows], -1).reshape(devices, cap_host)
    host_owner = jnp.where(host_valid, host_src, -1)
    inter_src = slot_sources(inter_device.reshape(-1), blocks * INTERS, cap_inter, devices)
    inter_valid = inter_src >= 0
    inter_rows = jnp.maximum(inter_src, 0)
    inter_target = jnp.where(inter_valid, inter_slot.reshape(-1)[inter_rows], -1).reshape(
        devices, cap_inter
    )
    inter_owner = jnp.where(inter_valid, inter_src // INTERS, -1)
    inter_block = inter_rows // INTERS

    def operate(field):
        padded = with_halo(field, (("gx", 0), ("gy", 1)), 1)
        zero_plane = jnp.zeros_like(field[:, :, :1])
        beside = padded[2:, 1:-1] + padded[:-2, 1:-1] + padded[1:-1, 2:] + padded[1:-1, :-2]
        beside = beside + jnp.concatenate([field[:, :, 1:], zero_plane], 2)
        beside = beside + jnp.concatenate([zero_plane, field[:, :, :-1]], 2)
        stencil = (stored + 6.0) * field - beside
        tiles = field.reshape(blocks, width)
        send_tile = jnp.where(host_valid[:, None], tiles[host_rows], 0.0).reshape(
            devices, cap_host, width
        )
        inter_tile = jnp.where(inter_valid[:, None], tiles[inter_block], 0.0).reshape(
            devices, cap_inter, width
        )
        out_tile, out_col, got_inter, got_target = (
            lax.all_to_all(send_tile, ("gx", "gy"), split_axis=0, concat_axis=0, tiled=True),
            lax.all_to_all(host_cols, ("gx", "gy"), split_axis=0, concat_axis=0, tiled=True),
            lax.all_to_all(inter_tile, ("gx", "gy"), split_axis=0, concat_axis=0, tiled=True),
            lax.all_to_all(inter_target, ("gx", "gy"), split_axis=0, concat_axis=0, tiled=True),
        )
        flat_target = got_target.reshape(-1)
        flat_arrived = got_inter.reshape(-1, width)
        valid = flat_target >= 0
        gain = jnp.where(
            valid[:, None], TI * (tiles[jnp.maximum(flat_target, 0)] - flat_arrived), 0.0
        )
        gain, inter_added = (gain.reshape(got_inter.shape), scatter_rows(flat_target, gain, blocks))
        twin_tile, twin_brick = swapped((out_tile, tiles), "grp", 0)
        tile_in = jnp.where(is_frac, out_tile, twin_tile)
        column_in = jnp.where(is_frac, twin_brick, tiles)
        flux, mat_added = matrix_side(tile_in, out_col, column_in)
        flux_back, gain_back = (
            lax.all_to_all(flux, ("gx", "gy"), split_axis=0, concat_axis=0, tiled=True),
            lax.all_to_all(gain, ("gx", "gy"), split_axis=0, concat_axis=0, tiled=True),
        )
        frac_out = stored.reshape(blocks, width) * tiles + in_plane(tiles) + inter_added
        frac_out = frac_out - scatter_rows(host_owner, flux_back.reshape(-1, width), blocks)
        frac_out = frac_out - scatter_rows(inter_owner, gain_back.reshape(-1, width), blocks)
        mat_out = stencil + mat_added.reshape(bx_cells, by_cells, width)
        return jnp.where(is_frac, frac_out.reshape(bx_cells, by_cells, width), mat_out)

    theta = (LMAX + LMIN) / 2.0
    delta = (LMAX - LMIN) / 2.0
    sigma = theta / delta
    target_side = source[0]
    pressure = jnp.zeros_like(target_side)
    for sweep in range(SWEEPS):
        residual = target_side - operate(pressure)
        dirn = residual / (theta * diag)
        rho = 1.0 / sigma
        for inner in range(DEGREE):
            pressure = pressure + dirn
            residual = residual - operate(dirn)
            rho_new = 1.0 / (2.0 * sigma - rho)
            dirn = rho_new * rho * dirn + 2.0 * rho_new / delta * residual / diag
            rho = rho_new
        pressure = pressure + dirn
    return pressure[None]


def solution(mesh):
    in_specs = (
        P("grp", "gx", "gy", None),
        P("grp", "gx", "gy", None),
        P(("gx", "gy"), None),
        P(("gx", "gy")),
        P(("gx", "gy"), None),
        P(("gx", "gy"), None),
    )
    out_specs = P("grp", "gx", "gy", None)
    return jax.shard_map(
        per_device, mesh=mesh, in_specs=in_specs, out_specs=out_specs, check_vma=False
    )
```

profile of v0, /device:TPU:3, one launch (start us, length us, event | category | flops | bytes accessed | tf_op | source)
XLA Modules:
  0.0 917.4 jit_solution(7352881938668593071)
XLA Ops:
  4.8 14.8 %all-to-all-start.2 = ((s32[128,1,2]{2,1,0:T(1,128)}), s32[128,1,2]{2,1,0:T(1,128)S(1)}, u32[]{:S(2)}, u32[]{:S(2)}) async-start(s32[128,1,2]{2,1,0:T(1,128)} %bitcast.11), calls=%async_computation.2 | async-start | bytes 131072 | tf_op jit(solution)/shard_map/all_to_all | solution.py:118
  31.4 11.3 %all-to-all-start = ((s32[128,1,4]{2,1,0:T(1,128)}), s32[128,1,4]{2,1,0:T(1,128)S(1)}, u32[]{:S(2)}, u32[]{:S(2)}) async-start(s32[128,1,4]{2,1,0:T(1,128)} %bitcast.7), calls=%async_computation | async-start | bytes 131072 | tf_op jit(solution)/shard_map/all_to_all | solution.py:120
  43.7 11.0 %all-to-all-done = s32[128,1,4]{2,1,0:T(1,128)S(1)} async-done(((s32[128,1,4]{2,1,0:T(1,128)}), s32[128,1,4]{2,1,0:T(1,128)S(1)}, u32[]{:S(2)}, u32[]{:S(2)}) %all-to-all-start) | async-done | bytes 2080 | tf_op jit(solution)/shard_map/all_to_all | solution.py:120
  64.8 11.2 %all-to-all-done.3 = f32[128,2,256]{2,1,0:T(2,128)S(1)} async-done(((f32[128,2,256]{2,1,0:T(2,128)}), f32[128,2,256]{2,1,0:T(2,128)S(1)}, u32[]{:S(2)}, u32[]{:S(2)}) %all-to-all-start.3) | async-done | bytes 262176 | tf_op jit(solution)/shard_map/all_to_all | solution.py:117
  115.1 12.1 %all-to-all-done.4 = f32[128,2,256]{2,1,0:T(2,128)S(1)} async-done(((f32[128,2,256]{2,1,0:T(2,128)}), f32[128,2,256]{2,1,0:T(2,128)S(1)}, u32[]{:S(2)}, u32[]{:S(2)}) %all-to-all-start.4) | async-done | bytes 262176 | tf_op jit(solution)/shard_map/all_to_all | solution.py:134
  159.2 13.7 %all-to-all-start.7 = ((f32[128,2,256]{2,1,0:T(2,128)}), f32[128,2,256]{2,1,0:T(2,128)S(1)}, u32[]{:S(2)}, u32[]{:S(2)}) async-start(f32[128,2,256]{2,1,0:T(2,128)} %broadcast_select_fusion.14), calls=%async_computation.7 | async-start | bytes 524288 | tf_op jit(solution)/shard_map/all_to_all | solution.py:117
  175.6 12.5 %all-to-all-done.7 = f32[128,2,256]{2,1,0:T(2,128)S(1)} async-done(((f32[128,2,256]{2,1,0:T(2,128)}), f32[128,2,256]{2,1,0:T(2,128)S(1)}, u32[]{:S(2)}, u32[]{:S(2)}) %all-to-all-start.7) | async-done | bytes 262176 | tf_op jit(solution)/shard_map/all_to_all | solution.py:117
  216.0 9.7 %all-to-all-start.8 = ((f32[128,2,256]{2,1,0:T(2,128)}), f32[128,2,256]{2,1,0:T(2,128)S(1)}, u32[]{:S(2)}, u32[]{:S(2)}) async-start(f32[128,2,256]{2,1,0:T(2,128)} %multiply_select_fusion.6), calls=%async_computation.8 | async-start | bytes 524288 | tf_op jit(solution)/shard_map/all_to_all | solution.py:134
  256.7 12.0 %all-to-all-done.9 = f32[128,4,256]{2,1,0:T(4,128)S(1)} async-done(((f32[128,4,256]{2,1,0:T(4,128)}), f32[128,4,256]{2,1,0:T(4,128)S(1)}, u32[]{:S(2)}, u32[]{:S(2)}) %all-to-all-start.9) | async-done | bytes 524320 | tf_op jit(solution)/shard_map/all_to_all | solution.py:135
  283.3 12.6 %all-to-all-done.11 = f32[128,2,256]{2,1,0:T(2,128)S(1)} async-done(((f32[128,2,256]{2,1,0:T(2,128)}), f32[128,2,256]{2,1,0:T(2,128)S(1)}, u32[]{:S(2)}, u32[]{:S(2)}) %all-to-all-start.11) | async-done | bytes 262176 | tf_op jit(solution)/shard_map/all_to_all | solution.py:117
  323.7 9.4 %all-to-all-start.12 = ((f32[128,2,256]{2,1,0:T(2,128)}), f32[128,2,256]{2,1,0:T(2,128)S(1)}, u32[]{:S(2)}, u32[]{:S(2)}) async-start(f32[128,2,256]{2,1,0:T(2,128)} %multiply_select_fusion.5), calls=%async_computation.12 | async-start | bytes 524288 | tf_op jit(solution)/shard_map/all_to_all | solution.py:134
  364.9 11.4 %all-to-all-done.13 = f32[128,4,256]{2,1,0:T(4,128)S(1)} async-done(((f32[128,4,256]{2,1,0:T(4,128)}), f32[128,4,256]{2,1,0:T(4,128)S(1)}, u32[]{:S(2)}, u32[]{:S(2)}) %all-to-all-start.13) | async-done | bytes 524320 | tf_op jit(solution)/shard_map/all_to_all | solution.py:135
  390.8 12.6 %all-to-all-done.15 = f32[128,2,256]{2,1,0:T(2,128)S(1)} async-done(((f32[128,2,256]{2,1,0:T(2,128)}), f32[128,2,256]{2,1,0:T(2,128)S(1)}, u32[]{:S(2)}, u32[]{:S(2)}) %all-to-all-start.15) | async-done | bytes 262176 | tf_op jit(solution)/shard_map/all_to_all | solution.py:117
  473.8 10.0 %all-to-all-done.17 = f32[128,4,256]{2,1,0:T(4,128)S(1)} async-done(((f32[128,4,256]{2,1,0:T(4,128)}), f32[128,4,256]{2,1,0:T(4,128)S(1)}, u32[]{:S(2)}, u32[]{:S(2)}) %all-to-all-start.17) | async-done | bytes 524320 | tf_op jit(solution)/shard_map/all_to_all | solution.py:135
  498.0 12.6 %all-to-all-done.19 = f32[128,2,256]{2,1,0:T(2,128)S(1)} async-done(((f32[128,2,256]{2,1,0:T(2,128)}), f32[128,2,256]{2,1,0:T(2,128)S(1)}, u32[]{:S(2)}, u32[]{:S(2)}) %all-to-all-start.19) | async-done | bytes 262176 | tf_op jit(solution)/shard_map/all_to_all | solution.py:117
  538.4 9.4 %all-to-all-start.20 = ((f32[128,2,256]{2,1,0:T(2,128)}), f32[128,2,256]{2,1,0:T(2,128)S(1)}, u32[]{:S(2)}, u32[]{:S(2)}) async-start(f32[128,2,256]{2,1,0:T(2,128)} %multiply_select_fusion.3), calls=%async_computation.20 | async-start | bytes 524288 | tf_op jit(solution)/shard_map/all_to_all | solution.py:134
  580.0 10.9 %all-to-all-done.21 = f32[128,4,256]{2,1,0:T(4,128)S(1)} async-done(((f32[128,4,256]{2,1,0:T(4,128)}), f32[128,4,256]{2,1,0:T(4,128)S(1)}, u32[]{:S(2)}, u32[]{:S(2)}) %all-to-all-start.21) | async-done | bytes 524320 | tf_op jit(solution)/shard_map/all_to_all | solution.py:135
  605.5 12.6 %all-to-all-done.23 = f32[128,2,256]{2,1,0:T(2,128)S(1)} async-done(((f32[128,2,256]{2,1,0:T(2,128)}), f32[128,2,256]{2,1,0:T(2,128)S(1)}, u32[]{:S(2)}, u32[]{:S(2)}) %all-to-all-start.23) | async-done | bytes 262176 | tf_op jit(solution)/shard_map/all_to_all | solution.py:117
  646.0 9.6 %all-to-all-start.24 = ((f32[128,2,256]{2,1,0:T(2,128)}), f32[128,2,256]{2,1,0:T(2,128)S(1)}, u32[]{:S(2)}, u32[]{:S(2)}) async-start(f32[128,2,256]{2,1,0:T(2,128)} %multiply_select_fusion.2), calls=%async_computation.24 | async-start | bytes 524288 | tf_op jit(solution)/shard_map/all_to_all | solution.py:134
  687.3 11.4 %all-to-all-done.25 = f32[128,4,256]{2,1,0:T(4,128)S(1)} async-done(((f32[128,4,256]{2,1,0:T(4,128)}), f32[128,4,256]{2,1,0:T(4,128)S(1)}, u32[]{:S(2)}, u32[]{:S(2)}) %all-to-all-start.25) | async-done | bytes 524320 | tf_op jit(solution)/shard_map/all_to_all | solution.py:135
  713.2 12.6 %all-to-all-done.27 = f32[128,2,256]{2,1,0:T(2,128)S(1)} async-done(((f32[128,2,256]{2,1,0:T(2,128)}), f32[128,2,256]{2,1,0:T(2,128)S(1)}, u32[]{:S(2)}, u32[]{:S(2)}) %all-to-all-start.27) | async-done | bytes 262176 | tf_op jit(solution)/shard_map/all_to_all | solution.py:117
  794.8 11.3 %all-to-all-done.29 = f32[128,4,256]{2,1,0:T(4,128)S(1)} async-done(((f32[128,4,256]{2,1,0:T(4,128)}), f32[128,4,256]{2,1,0:T(4,128)S(1)}, u32[]{:S(2)}, u32[]{:S(2)}) %all-to-all-start.29) | async-done | bytes 524320 | tf_op jit(solution)/shard_map/all_to_all | solution.py:135
  820.7 12.6 %all-to-all-done.31 = f32[128,2,256]{2,1,0:T(2,128)S(1)} async-done(((f32[128,2,256]{2,1,0:T(2,128)}), f32[128,2,256]{2,1,0:T(2,128)S(1)}, u32[]{:S(2)}, u32[]{:S(2)}) %all-to-all-start.31) | async-done | bytes 262176 | tf_op jit(solution)/shard_map/all_to_all | solution.py:117
  902.7 11.1 %all-to-all-done.33 = f32[128,4,256]{2,1,0:T(4,128)S(1)} async-done(((f32[128,4,256]{2,1,0:T(4,128)}), f32[128,4,256]{2,1,0:T(4,128)S(1)}, u32[]{:S(2)}, u32[]{:S(2)}) %all-to-all-start.33) | async-done | bytes 524320 | tf_op jit(solution)/shard_map/all_to_all | solution.py:135
  (497 shorter events, 636.3 us)
Async XLA Ops:
  4.8 26.6 %all-to-all-start.2 = ((s32[128,1,2]{2,1,0:T(1,128)}), s32[128,1,2]{2,1,0:T(1,128)S(1)}, u32[]{:S(2)}, u32[]{:S(2)}) async-start(s32[128,1,2]{2,1,0:T(1,128)} %bitcast.11), calls=%async_computation.2 | async-start | bytes 131072 | tf_op jit(solution)/shard_map/all_to_all | solution.py:118
  60.7 27.0 %collective-permute-start = (f32[128,256]{1,0:T(8,128)S(1)}, f32[128,256]{1,0:T(8,128)S(1)}, u32[]{:S(2)}, u32[]{:S(2)}) collective-permute-start(f32[128,256]{1,0:T(8,128)S(1)} %select_n.456), channel_id=1, source_target_pairs={{0,128},{128,0},{1,129},{129,1},{2,130},{130,2},{3,131},{131,3},{4... | collective-permute-start | bytes 393224 | tf_op jit(solution)/shard_map/ppermute | solution.py:39
  76.0 28.3 %all-to-all-start.1 = ((f32[128,4,256]{2,1,0:T(4,128)}), f32[128,4,256]{2,1,0:T(4,128)S(1)}, u32[]{:S(2)}, u32[]{:S(2)}) async-start(f32[128,4,256]{2,1,0:T(4,128)} %broadcast_select_fusion.7), calls=%async_computation.1 | async-start | bytes 1048576 | tf_op jit(solution)/shard_map/all_to_all | solution.py:119
  127.2 27.9 %all-to-all-start.5 = ((f32[128,4,256]{2,1,0:T(4,128)}), f32[128,4,256]{2,1,0:T(4,128)S(1)}, u32[]{:S(2)}, u32[]{:S(2)}) async-start(f32[128,4,256]{2,1,0:T(4,128)} %subtract_select_fusion.7), calls=%async_computation.5 | async-start | bytes 1048576 | tf_op jit(solution)/shard_map/all_to_all | solution.py:135
  159.2 28.9 %all-to-all-start.7 = ((f32[128,2,256]{2,1,0:T(2,128)}), f32[128,2,256]{2,1,0:T(2,128)S(1)}, u32[]{:S(2)}, u32[]{:S(2)}) async-start(f32[128,2,256]{2,1,0:T(2,128)} %broadcast_select_fusion.14), calls=%async_computation.7 | async-start | bytes 524288 | tf_op jit(solution)/shard_map/all_to_all | solution.py:117
  188.1 27.9 %all-to-all-start.6 = ((f32[128,4,256]{2,1,0:T(4,128)}), f32[128,4,256]{2,1,0:T(4,128)S(1)}, u32[]{:S(2)}, u32[]{:S(2)}) async-start(f32[128,4,256]{2,1,0:T(4,128)} %broadcast_select_fusion.6), calls=%async_computation.6 | async-start | bytes 1048576 | tf_op jit(solution)/shard_map/all_to_all | solution.py:119
  216.0 24.8 %all-to-all-start.8 = ((f32[128,2,256]{2,1,0:T(2,128)}), f32[128,2,256]{2,1,0:T(2,128)S(1)}, u32[]{:S(2)}, u32[]{:S(2)}) async-start(f32[128,2,256]{2,1,0:T(2,128)} %multiply_select_fusion.6), calls=%async_computation.8 | async-start | bytes 524288 | tf_op jit(solution)/shard_map/all_to_all | solution.py:134
  240.8 28.0 %all-to-all-start.9 = ((f32[128,4,256]{2,1,0:T(4,128)}), f32[128,4,256]{2,1,0:T(4,128)S(1)}, u32[]{:S(2)}, u32[]{:S(2)}) async-start(f32[128,4,256]{2,1,0:T(4,128)} %subtract_select_fusion.6), calls=%async_computation.9 | async-start | bytes 1048576 | tf_op jit(solution)/shard_map/all_to_all | solution.py:135
  295.9 27.9 %all-to-all-start.10 = ((f32[128,4,256]{2,1,0:T(4,128)}), f32[128,4,256]{2,1,0:T(4,128)S(1)}, u32[]{:S(2)}, u32[]{:S(2)}) async-start(f32[128,4,256]{2,1,0:T(4,128)} %broadcast_select_fusion.5), calls=%async_computation.10 | async-start | bytes 1048576 | tf_op jit(solution)/shard_map/all_to_all | solution.py:119
  323.7 24.7 %all-to-all-start.12 = ((f32[128,2,256]{2,1,0:T(2,128)}), f32[128,2,256]{2,1,0:T(2,128)S(1)}, u32[]{:S(2)}, u32[]{:S(2)}) async-start(f32[128,2,256]{2,1,0:T(2,128)} %multiply_select_fusion.5), calls=%async_computation.12 | async-start | bytes 524288 | tf_op jit(solution)/shard_map/all_to_all | solution.py:134
  348.4 27.9 %all-to-all-start.13 = ((f32[128,4,256]{2,1,0:T(4,128)}), f32[128,4,256]{2,1,0:T(4,128)S(1)}, u32[]{:S(2)}, u32[]{:S(2)}) async-start(f32[128,4,256]{2,1,0:T(4,128)} %subtract_select_fusion.5), calls=%async_computation.13 | async-start | bytes 1048576 | tf_op jit(solution)/shard_map/all_to_all | solution.py:135
  403.3 28.0 %all-to-all-start.14 = ((f32[128,4,256]{2,1,0:T(4,128)}), f32[128,4,256]{2,1,0:T(4,128)S(1)}, u32[]{:S(2)}, u32[]{:S(2)}) async-start(f32[128,4,256]{2,1,0:T(4,128)} %broadcast_select_fusion.4), calls=%async_computation.14 | async-start | bytes 1048576 | tf_op jit(solution)/shard_map/all_to_all | solution.py:119
  456.0 27.9 %all-to-all-start.17 = ((f32[128,4,256]{2,1,0:T(4,128)}), f32[128,4,256]{2,1,0:T(4,128)S(1)}, u32[]{:S(2)}, u32[]{:S(2)}) async-start(f32[128,4,256]{2,1,0:T(4,128)} %subtract_select_fusion.4), calls=%async_computation.17 | async-start | bytes 1048576 | tf_op jit(solution)/shard_map/all_to_all | solution.py:135
  510.6 27.9 %all-to-all-start.18 = ((f32[128,4,256]{2,1,0:T(4,128)}), f32[128,4,256]{2,1,0:T(4,128)S(1)}, u32[]{:S(2)}, u32[]{:S(2)}) async-start(f32[128,4,256]{2,1,0:T(4,128)} %broadcast_select_fusion.3), calls=%async_computation.18 | async-start | bytes 1048576 | tf_op jit(solution)/shard_map/all_to_all | solution.py:119
  538.4 24.7 %all-to-all-start.20 = ((f32[128,2,256]{2,1,0:T(2,128)}), f32[128,2,256]{2,1,0:T(2,128)S(1)}, u32[]{:S(2)}, u32[]{:S(2)}) async-start(f32[128,2,256]{2,1,0:T(2,128)} %multiply_select_fusion.3), calls=%async_computation.20 | async-start | bytes 524288 | tf_op jit(solution)/shard_map/all_to_all | solution.py:134
  563.1 27.9 %all-to-all-start.21 = ((f32[128,4,256]{2,1,0:T(4,128)}), f32[128,4,256]{2,1,0:T(4,128)S(1)}, u32[]{:S(2)}, u32[]{:S(2)}) async-start(f32[128,4,256]{2,1,0:T(4,128)} %subtract_select_fusion.3), calls=%async_computation.21 | async-start | bytes 1048576 | tf_op jit(solution)/shard_map/all_to_all | solution.py:135
  618.1 27.9 %all-to-all-start.22 = ((f32[128,4,256]{2,1,0:T(4,128)}), f32[128,4,256]{2,1,0:T(4,128)S(1)}, u32[]{:S(2)}, u32[]{:S(2)}) async-start(f32[128,4,256]{2,1,0:T(4,128)} %broadcast_select_fusion.2), calls=%async_computation.22 | async-start | bytes 1048576 | tf_op jit(solution)/shard_map/all_to_all | solution.py:119
  646.0 24.8 %all-to-all-start.24 = ((f32[128,2,256]{2,1,0:T(2,128)}), f32[128,2,256]{2,1,0:T(2,128)S(1)}, u32[]{:S(2)}, u32[]{:S(2)}) async-start(f32[128,2,256]{2,1,0:T(2,128)} %multiply_select_fusion.2), calls=%async_computation.24 | async-start | bytes 524288 | tf_op jit(solution)/shard_map/all_to_all | solution.py:134
  670.7 28.0 %all-to-all-start.25 = ((f32[128,4,256]{2,1,0:T(4,128)}), f32[128,4,256]{2,1,0:T(4,128)S(1)}, u32[]{:S(2)}, u32[]{:S(2)}) async-start(f32[128,4,256]{2,1,0:T(4,128)} %subtract_select_fusion.2), calls=%async_computation.25 | async-start | bytes 1048576 | tf_op jit(solution)/shard_map/all_to_all | solution.py:135
  725.8 27.9 %all-to-all-start.26 = ((f32[128,4,256]{2,1,0:T(4,128)}), f32[128,4,256]{2,1,0:T(4,128)S(1)}, u32[]{:S(2)}, u32[]{:S(2)}) async-start(f32[128,4,256]{2,1,0:T(4,128)} %broadcast_select_fusion.1), calls=%async_computation.26 | async-start | bytes 1048576 | tf_op jit(solution)/shard_map/all_to_all | solution.py:119
  753.6 24.7 %all-to-all-start.28 = ((f32[128,2,256]{2,1,0:T(2,128)}), f32[128,2,256]{2,1,0:T(2,128)S(1)}, u32[]{:S(2)}, u32[]{:S(2)}) async-start(f32[128,2,256]{2,1,0:T(2,128)} %multiply_select_fusion.1), calls=%async_computation.28 | async-start | bytes 524288 | tf_op jit(solution)/shard_map/all_to_all | solution.py:134
  778.3 27.9 %all-to-all-start.29 = ((f32[128,4,256]{2,1,0:T(4,128)}), f32[128,4,256]{2,1,0:T(4,128)S(1)}, u32[]{:S(2)}, u32[]{:S(2)}) async-start(f32[128,4,256]{2,1,0:T(4,128)} %subtract_select_fusion.1), calls=%async_computation.29 | async-start | bytes 1048576 | tf_op jit(solution)/shard_map/all_to_all | solution.py:135
  833.3 28.1 %all-to-all-start.30 = ((f32[128,4,256]{2,1,0:T(4,128)}), f32[128,4,256]{2,1,0:T(4,128)S(1)}, u32[]{:S(2)}, u32[]{:S(2)}) async-start(f32[128,4,256]{2,1,0:T(4,128)} %broadcast_select_fusion), calls=%async_computation.30 | async-start | bytes 1048576 | tf_op jit(solution)/shard_map/all_to_all | solution.py:119
  886.0 27.9 %all-to-all-start.33 = ((f32[128,4,256]{2,1,0:T(4,128)}), f32[128,4,256]{2,1,0:T(4,128)S(1)}, u32[]{:S(2)}, u32[]{:S(2)}) async-start(f32[128,4,256]{2,1,0:T(4,128)} %subtract_select_fusion), calls=%async_computation.33 | async-start | bytes 1048576 | tf_op jit(solution)/shard_map/all_to_all | solution.py:135
  (104 other events, 1056.6 us)
where the time goes:
time: 932 us; the launch traced here: 917 us
  waiting for transfers between devices  393 us (42%)
  starting transfers between devices  370 us (40%)
  local copies, waits for them, and re-layouts  91.6 us (10%)
  other arithmetic  39 us (4%)
  matrix products  20.9 us (2%)
    all_to_all x8, waiting for transfers between devices, operate(): lax.all_to_all(send_tile, ('gx', 'gy'), split_axis=0, concat_axis=0, tile...  99.1 us
    ppermute x16, waiting for transfers between devices, swapped(): lax.ppermute(value, axis, [(i, i ^ 1 << bit) for i in range(lax.axis_size...  93.9 us
    all_to_all x8, waiting for transfers between devices, operate(): lax.all_to_all(gain, ('gx', 'gy'), split_axis=0, concat_axis=0, tiled=True)  78.5 us
    all_to_all x8, starting transfers between devices, operate(): lax.all_to_all(flux, ('gx', 'gy'), split_axis=0, concat_axis=0, tiled=True)  73.8 us
    all_to_all x8, starting transfers between devices, operate(): lax.all_to_all(send_tile, ('gx', 'gy'), split_axis=0, concat_axis=0, tile...  60.3 us
    all_to_all x8, waiting for transfers between devices, operate(): lax.all_to_all(flux, ('gx', 'gy'), split_axis=0, concat_axis=0, tiled=True)  59.2 us
    all_to_all x8, starting transfers between devices, operate(): lax.all_to_all(gain, ('gx', 'gy'), split_axis=0, concat_axis=0, tiled=True)  55.4 us
    all_to_all x8, starting transfers between devices, operate(): lax.all_to_all(inter_tile, ('gx', 'gy'), split_axis=0, concat_axis=0, til...  55.4 us
  transfers between devices with their start and end apart: 82, of which 50 were waited for; matrix products, arithmetic and copies ran while one was open for 12% of the time, Pallas kernels for 0%

commit v1 on v0

v1 whole, which is shorter than its diff:
```python
import jax
import jax.numpy as jnp
from jax import lax
from jax.experimental import pallas as pl
from jax.experimental.pallas import tpu as pltpu
from jax.sharding import PartitionSpec as P

TF = 2.0
TI = 1.0
TM = 0.5
LMIN = 0.3
LMAX = 3.0
STEPS = 7

ROWS = 512
PEERS = 32
MSG = 48

F32 = jnp.float32
BF16 = jnp.bfloat16
I32 = jnp.int32
MESH = pl.DeviceIdType.MESH


def coefficients():
    theta = (LMAX + LMIN) / 2.0
    delta = (LMAX - LMIN) / 2.0
    sigma = theta / delta
    rho = 1.0 / sigma
    pairs = []
    for _ in range(3):
        rho_new = 1.0 / (2.0 * sigma - rho)
        pairs.append((rho_new * rho, 2.0 * rho_new / delta))
        rho = rho_new
    pairs.append((0.0, 1.0 / theta))
    return pairs, theta


def turn(x, shift):
    shift = shift % 128
    return x if shift == 0 else pltpu.roll(x, shift, 1)


def lanes(rows):
    return lax.broadcasted_iota(I32, (rows, 128), 1)


def kernel(
    src, sto, gbf, gbm, sbf, sbm, out,
    gf, gm, sf, sm, wf, wm, rf, rm,
    send, recv, hs, hz, ys, hy, hx,
    tx, rx, tx2, rx2,
    d_ref, r_ref, p_ref, c_ref, i_ref,
    send_sem, recv_sem, hsend_sem, hrecv_sem, tsend_sem, trecv_sem, usend_sem, urecv_sem,
):
    g = lax.axis_index("grp")
    gx = lax.axis_index("gx")
    gy = lax.axis_index("gy")
    x_hi = gx // 16
    cz = (gx // 2) % 8
    core = gx % 2
    w = x_hi * 4 + g * 2 + core

    def place(w_, y_, z_):
        return ((w_ // 2) % 2, (w_ // 4) * 16 + z_ * 2 + w_ % 2, y_)

    def peer(k):
        return place((w + k // 4) % 8, (gy + k % 4) % 4, cz)

    w_home = gx // 4
    u_home = gx % 4
    own = w_home == w

    barrier = pltpu.get_barrier_semaphore()

    def greet(device):
        pl.semaphore_signal(barrier, inc=1, device_id=device, device_id_type=MESH)

    def greet_peer(k, carry):
        greet(peer(k))
        return carry

    lax.fori_loop(1, PEERS, greet_peer, 0)
    greet(place(w, gy, (cz + 1) % 8))
    greet(place(w, gy, (cz + 7) % 8))

    def greet_far(n, carry):
        @pl.when(jnp.logical_not(own & (n == cz)))
        def _():
            greet(place(w_home, gy, n))

        @pl.when(jnp.logical_not(own & (n == g * 4 + u_home)))
        def _():
            greet((n // 4, w * 4 + n % 4, gy))

        return carry

    lax.fori_loop(0, 8, greet_far, 0)

    l32 = lanes(32)
    for z in range(8):
        half, part = z // 4, z % 4
        for a, ref in ((0, src), (1, sto)):
            acc = jnp.zeros((32, 128), F32)
            for q in range(4):
                piece = ref[q * 32:(q + 1) * 32, half * 128:(half + 1) * 128]
                acc = jnp.where(l32 // 32 == q, turn(piece, 32 * (q - part)), acc)
            tx[z, a * 32:(a + 1) * 32, :] = acc

    pl.semaphore_wait(barrier, PEERS - 1 + 2 + jnp.where(own, 14, 16))

    def far_copy(z):
        return pltpu.make_async_remote_copy(
            src_ref=tx.at[z],
            dst_ref=rx.at[g * 4 + u_home],
            send_sem=tsend_sem.at[z],
            recv_sem=trecv_sem.at[g * 4 + u_home],
            device_id=place(w_home, gy, z),
            device_id_type=MESH,
        )

    def far_start(z, carry):
        mine = own & (z == cz)

        @pl.when(mine)
        def _():
            rx[g * 4 + u_home] = tx[z]

        @pl.when(jnp.logical_not(mine))
        def _():
            far_copy(z).start()

        return carry

    lax.fori_loop(0, 8, far_start, 0)

    iota_cols = lax.broadcasted_iota(I32, (80, ROWS), 1)

    def build_g(j, carry):
        at = pl.multiple_of(j * 80, 80)
        rows = gbf[pl.ds(at, 80), :]
        for q in range(4):
            hit = rows[:, q:q + 1] == iota_cols
            gf[pl.ds(at, 80), q * ROWS:(q + 1) * ROWS] = jnp.where(hit, 1.0, 0.0).astype(BF16)
        at = pl.multiple_of(j * 16, 16)
        rows = gbm[pl.ds(at, 16), :]
        for q in range(4):
            hit = rows[:, q:q + 1] == iota_cols[:16]
            gm[pl.ds(at, 16), q * ROWS:(q + 1) * ROWS] = jnp.where(hit, 1.0, 0.0).astype(BF16)
        return carry

    lax.fori_loop(0, 16, build_g, 0)

    within = lax.broadcasted_iota(I32, (1, 1280), 1) % 40
    weight = jnp.where(within < 32, TI, TM)

    def build_s(j, carry):
        at = pl.multiple_of(j * 16, 16)
        block = lax.broadcasted_iota(I32, (16, 1280), 0) + at
        for q in range(4):
            sf[pl.ds(at + q * ROWS, 16), :] = jnp.where(sbf[q:q + 1, :] == block, weight, 0.0).astype(BF16)
            sm[pl.ds(at + q * ROWS, 16), :] = jnp.where(
                sbm[q:q + 1, :] == block[:, :256], TM, 0.0
            ).astype(BF16)
        return carry

    lax.fori_loop(0, 32, build_s, 0)

    ln = lanes(ROWS)
    group = ln // 32
    is_f = ln < 32
    is_m = group == 1

    entering = jnp.where(lax.broadcasted_iota(I32, (1280, 128), 0) % 40 < 16, 1.0, 0.0).astype(BF16)
    ones = jnp.ones((256, 128), BF16)
    indeg = jnp.zeros((ROWS, 128), F32)
    hosted = jnp.zeros((ROWS, 128), F32)
    for q in range(4):
        indeg = indeg + jnp.dot(sf[q * ROWS:(q + 1) * ROWS, :], entering, preferred_element_type=F32)
        hosted = hosted + jnp.dot(sm[q * ROWS:(q + 1) * ROWS, :], ones, preferred_element_type=F32)

    def far_wait(n, carry):
        mine = own & (n == g * 4 + u_home)

        @pl.when(jnp.logical_not(mine))
        def _():
            pltpu.make_async_copy(rx.at[n], rx.at[n], trecv_sem.at[n]).wait()

        @pl.when(jnp.logical_not(own & (n == cz)))
        def _():
            pltpu.make_async_copy(tx.at[n], tx.at[n], tsend_sem.at[n]).wait()

        return carry

    lax.fori_loop(0, 8, far_wait, 0)

    pairs, theta = coefficients()
    for a, ref in ((0, r_ref), (1, c_ref)):
        for u in range(4):
            fr = rx[4 + u, a * 32:(a + 1) * 32, :]
            ma = rx[u, a * 32:(a + 1) * 32, :]
            for q in range(4):
                ref[u * 128 + q * 32:u * 128 + (q + 1) * 32, :] = jnp.where(
                    l32 < 32,
                    turn(fr, -32 * q),
                    jnp.where(l32 // 32 == 1, turn(ma, 32 - 32 * q), 0.0),
                )
    stored = c_ref[...]
    inverse = 1.0 / (stored + jnp.where(is_f, 4.0 * TF + 4.0 * TI + TM, 6.0 + TM))
    i_ref[...] = inverse
    c_ref[...] = stored + jnp.where(is_f, 4.0 * TF + 2.0 * TI + TM + indeg, 6.0 + hosted)
    d_ref[...] = r_ref[...] * inverse * (1.0 / theta)
    p_ref[...] = jnp.zeros((ROWS, 128), F32)

    low = jnp.where(cz > 0, 1.0, 0.0)
    high = jnp.where(cz < 7, 1.0, 0.0)
    left = jnp.where(w > 0, 1.0, 0.0)
    right = jnp.where(w < 7, 1.0, 0.0)
    near = jnp.where(gy > 0, 1.0, 0.0)
    beyond = jnp.where(gy < 3, 1.0, 0.0)
    l128 = lanes(128)

    def packed(x):
        acc = x[0:128]
        for q in range(1, 4):
            acc = jnp.where(l128 // 32 == q, turn(x[q * 128:(q + 1) * 128], 32 * q), acc)
        return acc

    def unpacked(x):
        return jnp.concatenate([turn(x, -32 * q) for q in range(4)], axis=0)

    def step(t, carry):
        par = t % 2

        def halo(n, source, dest, device):
            return pltpu.make_async_remote_copy(
                src_ref=source,
                dst_ref=dest,
                send_sem=hsend_sem.at[n],
                recv_sem=hrecv_sem.at[par, n],
                device_id=device,
                device_id_type=MESH,
            )

        halos = [
            halo(0, hs.at[0], hz.at[par, 0], place(w, gy, (cz + 1) % 8)),
            halo(1, hs.at[1], hz.at[par, 1], place(w, gy, (cz + 7) % 8)),
            halo(2, ys.at[1], hy.at[par, 0], place(w, (gy + 1) % 4, cz)),
            halo(3, ys.at[0], hy.at[par, 1], place(w, (gy + 3) % 4, cz)),
            halo(4, d_ref.at[pl.ds(ROWS - 8, 8)], hx.at[par, 0], place((w + 1) % 8, gy, cz)),
            halo(5, d_ref.at[pl.ds(0, 8)], hx.at[par, 1], place((w + 7) % 8, gy, cz)),
        ]
        d = d_ref[...]
        high_part = d.astype(BF16).astype(F32)
        low_part = d - high_part
        for s in range(4):
            for part, x in ((0, turn(high_part, 32 * s)), (1, turn(low_part, 32 * s))):
                q = (s + 1) % 4
                wf[s * ROWS:(s + 1) * ROWS, part * 128:(part + 1) * 128] = jnp.where(
                    group == s, x, 0.0
                ).astype(BF16)
                wm[q * ROWS:(q + 1) * ROWS, part * 128:(part + 1) * 128] = jnp.where(
                    group == q, x, 0.0
                ).astype(BF16)

        def message(k):
            return pltpu.make_async_remote_copy(
                src_ref=send.at[k],
                dst_ref=recv.at[par, k],
                send_sem=send_sem,
                recv_sem=recv_sem.at[par],
                device_id=peer(k),
                device_id_type=MESH,
            )

        def gather(c, carry):
            at = pl.multiple_of(c * 320, 320)
            x = jnp.dot(gf[pl.ds(at, 320), :], wf[...], preferred_element_type=F32)
            send[pl.ds(c * 8, 8), 0:40, :] = (x[:, :128] + x[:, 128:]).reshape(8, 40, 128)
            at = pl.multiple_of(c * 64, 64)
            x = jnp.dot(gm[pl.ds(at, 64), :], wm[...], preferred_element_type=F32)
            send[pl.ds(c * 8, 8), 40:48, :] = (x[:, :128] + x[:, 128:]).reshape(8, 8, 128)
            for n in range(8):
                k = c * 8 + n
                if n == 0:
                    @pl.when(c > 0)
                    def _():
                        message(k).start()
                else:
                    message(k).start()
            return carry

        hs[0] = packed(jnp.where(ln < 16, turn(d, -16), turn(d, -47)))
        hs[1] = packed(jnp.where(ln < 16, d, turn(d, -16)))
        ys[0] = d_ref[pl.ds(0, 64, stride=8), :]
        ys[1] = d_ref[pl.ds(7, 64, stride=8), :]
        for copy in halos:
            copy.start()
        lax.fori_loop(0, 4, gather, 0)
        recv[par, 0] = send[0]

        col = ln % 16
        before = turn(d, 1)
        after = turn(d, -1)
        nb_f = jnp.where(col != 0, before, 0.0) + jnp.where(col != 15, after, 0.0)
        nb_f = nb_f + jnp.where(ln >= 16, turn(d, 16), 0.0) + jnp.where(ln < 16, turn(d, -16), 0.0)
        nb_m = jnp.where(ln != 32, before, 0.0) + jnp.where(ln != 63, after, 0.0)
        nb_m = nb_m + jnp.concatenate([jnp.zeros((8, 128), F32), d[:ROWS - 8]], axis=0)
        nb_m = nb_m + jnp.concatenate([d[8:], jnp.zeros((8, 128), F32)], axis=0)
        sub = lax.broadcasted_iota(I32, (ROWS, 128), 0) % 8
        nb_m = nb_m + jnp.where(sub != 0, pltpu.roll(d, 1, 0), 0.0)
        nb_m = nb_m + jnp.where(sub != 7, pltpu.roll(d, ROWS - 1, 0), 0.0)
        for copy in halos:
            copy.wait_recv()
        from_low = unpacked(hz[par, 0]) * low
        from_high = unpacked(hz[par, 1]) * high
        nb_f = nb_f + jnp.where(ln < 16, from_low, turn(from_high, 16))
        nb_m = nb_m + jnp.where(ln == 32, turn(from_low, 16), 0.0)
        nb_m = nb_m + jnp.where(ln == 63, turn(from_high, 47), 0.0)
        y0 = jnp.broadcast_to((hy[par, 0] * near)[:, None, :], (64, 8, 128)).reshape(ROWS, 128)
        y1 = jnp.broadcast_to((hy[par, 1] * beyond)[:, None, :], (64, 8, 128)).reshape(ROWS, 128)
        nb_m = nb_m + jnp.where(sub == 0, y0, 0.0) + jnp.where(sub == 7, y1, 0.0)
        nb_m = nb_m + jnp.concatenate(
            [hx[par, 0] * left, jnp.zeros((ROWS - 16, 128), F32), hx[par, 1] * right], axis=0
        )
        nb = jnp.where(is_f, TF * nb_f, jnp.where(is_m, nb_m, 0.0))
        p_ref[...] = p_ref[...] + d
        r_ref[...] = r_ref[...] - (c_ref[...] * d - nb)

        pltpu.make_async_copy(
            recv.at[par, pl.ds(1, PEERS - 1)], recv.at[par, pl.ds(1, PEERS - 1)], recv_sem.at[par]
        ).wait()
        x = recv[par, :, 8:48, :].reshape(1280, 128)
        hi = x.astype(BF16)
        rf[:, 0:128] = hi
        rf[:, 128:256] = (x - hi.astype(F32)).astype(BF16)
        x = recv[par, :, 0:8, :].reshape(256, 128)
        hi = x.astype(BF16)
        rm[:, 0:128] = hi
        rm[:, 128:256] = (x - hi.astype(F32)).astype(BF16)
        sum_f = jnp.zeros((ROWS, 128), F32)
        sum_m = jnp.zeros((ROWS, 128), F32)
        for q in range(4):
            x = jnp.dot(sf[q * ROWS:(q + 1) * ROWS, :], rf[...], preferred_element_type=F32)
            sum_f = jnp.where(group == q, x[:, :128] + x[:, 128:], sum_f)
            x = jnp.dot(sm[q * ROWS:(q + 1) * ROWS, :], rm[...], preferred_element_type=F32)
            sum_m = jnp.where(group == q, x[:, :128] + x[:, 128:], sum_m)
        sum_f = sum_f + turn(sum_f, 64)
        sum_f = sum_f + turn(sum_f, 32)
        sum_m = sum_m + turn(sum_m, 64)
        sum_m = sum_m + turn(sum_m, 32)
        total = jnp.where(is_f, sum_f, jnp.where(is_m, sum_m, 0.0))

        for copy in halos:
            copy.wait_send()
        pltpu.make_async_copy(
            send.at[pl.ds(1, PEERS - 1)], send.at[pl.ds(1, PEERS - 1)], send_sem
        ).wait()
        phase = t % 4
        alpha = jnp.float32(pairs[3][0])
        beta = jnp.float32(pairs[3][1])
        for n in range(3):
            alpha = jnp.where(phase == n, jnp.float32(pairs[n][0]), alpha)
            beta = jnp.where(phase == n, jnp.float32(pairs[n][1]), beta)
        r = r_ref[...] + total
        r_ref[...] = r
        d_ref[...] = alpha * d_ref[...] + beta * (r * i_ref[...])
        return carry

    lax.fori_loop(0, STEPS, step, 0)

    for n in range(8):
        acc = jnp.zeros((32, 128), F32)
        for q in range(4):
            at = (n % 4) * 128 + q * 32
            piece = p_ref[at:at + 32, :] + d_ref[at:at + 32, :]
            acc = jnp.where(l32 // 32 == q, turn(piece, 32 * q - (32 if n < 4 else 0)), acc)
        tx2[n] = acc

    def back_start(n, carry):
        mine = own & (n == g * 4 + u_home)

        @pl.when(mine)
        def _():
            rx2[cz] = tx2[n]

        @pl.when(jnp.logical_not(mine))
        def _():
            pltpu.make_async_remote_copy(
                src_ref=tx2.at[n],
                dst_ref=rx2.at[cz],
                send_sem=usend_sem.at[n],
                recv_sem=urecv_sem.at[cz],
                device_id=(n // 4, w * 4 + n % 4, gy),
                device_id_type=MESH,
            ).start()

        return carry

    lax.fori_loop(0, 8, back_start, 0)

    def back_wait(n, carry):
        @pl.when(jnp.logical_not(own & (n == cz)))
        def _():
            pltpu.make_async_copy(rx2.at[n], rx2.at[n], urecv_sem.at[n]).wait()

        @pl.when(jnp.logical_not(own & (n == g * 4 + u_home)))
        def _():
            pltpu.make_async_copy(tx2.at[n], tx2.at[n], usend_sem.at[n]).wait()

        return carry

    lax.fori_loop(0, 8, back_wait, 0)
    for half in range(2):
        for q in range(4):
            acc = jnp.zeros((32, 128), F32)
            for part in range(4):
                acc = jnp.where(l32 // 32 == part, turn(rx2[half * 4 + part], 32 * (part - q)), acc)
            out[q * 32:(q + 1) * 32, half * 128:(half + 1) * 128] = acc


def edge_table(dest, where_to, per_row, most):
    count = dest.shape[0]
    order = jnp.arange(count, dtype=I32)
    same = (dest[:, None] == dest[None, :]) & (order[None, :] < order[:, None])
    rank = jnp.sum(same.astype(I32), axis=1)
    code = 1 + (order // per_row) * 128 + where_to
    key = rank * 128 + dest
    wanted = jnp.arange(most * 128, dtype=I32)
    return jnp.sum(jnp.where(key[None, :] == wanted[:, None], code[None, :], 0), axis=1).reshape(most, 128)


def tables(host_device, host_column, inter_device, inter_slot):
    g = lax.axis_index("grp")
    gx = lax.axis_index("gx")
    gy = lax.axis_index("gy")
    w = (gx // 16) * 4 + g * 2 + gx % 2
    mine = jnp.concatenate(
        [
            edge_table(inter_device.reshape(-1), inter_slot.reshape(-1), 2, 4),
            edge_table(host_device.reshape(-1), host_column, 1, 2),
        ],
        axis=0,
    )
    every = lax.all_gather(mine, ("gx", "gy"), axis=0, tiled=False).reshape(8, 4, 4, 6, 8, 4, 4)
    sent = lax.dynamic_slice(every, (w, 0, gy, 0, 0, 0, 0), (1, 4, 1, 6, 8, 4, 4)).reshape(4, 6, 8, 4, 4)
    came = lax.dynamic_slice(every, (0, 0, 0, 0, w, 0, gy), (8, 4, 4, 6, 1, 4, 1)).reshape(8, 4, 4, 6, 4)

    def relative(x):
        x = lax.dynamic_slice_in_dim(jnp.concatenate([x, x], axis=0), w, 8, axis=0)
        return lax.dynamic_slice_in_dim(jnp.concatenate([x, x], axis=1), gy, 4, axis=1)

    sent = relative(sent.transpose(2, 4, 0, 3, 1))
    came = relative(came.transpose(0, 2, 1, 4, 3))
    u = jnp.arange(4, dtype=I32) * 128
    sent = jnp.where(sent > 0, u[:, None, None] + (sent - 1) // 128, -1)
    came = jnp.where(came > 0, u[None, :, None] + (came - 1) % 128, -1)
    f_out = sent[..., :4].reshape(8, 4, 16, 4)
    h_out = sent[..., 4:].reshape(8, 4, 8, 4)
    f_in = came[..., :4].reshape(8, 4, 16, 4)
    h_in = came[..., 4:].reshape(8, 4, 8, 4)

    def mirror(x):
        x = jnp.concatenate([x[:1], x[:0:-1]], axis=0)
        return jnp.concatenate([x[:, :1], x[:, :0:-1]], axis=1)

    gbf = jnp.concatenate([h_out, f_out, f_in], axis=2).reshape(1280, 4)
    gbm = h_in.reshape(256, 4)
    sbf = mirror(jnp.concatenate([f_in, f_out, h_out], axis=2)).reshape(1280, 4).T
    sbm = mirror(h_in).reshape(256, 4).T
    return gbf, gbm, sbf, sbm


def per_device(source, storage, host_device, host_column, inter_device, inter_slot):
    gbf, gbm, sbf, sbm = tables(host_device, host_column, inter_device, inter_slot)
    dma = pltpu.SemaphoreType.DMA
    result = pl.pallas_call(
        kernel,
        out_shape=jax.ShapeDtypeStruct((128, 256), F32),
        in_specs=[pl.BlockSpec(memory_space=pltpu.VMEM)] * 6,
        out_specs=pl.BlockSpec(memory_space=pltpu.VMEM),
        scratch_shapes=[
            pltpu.VMEM((1280, 2048), BF16),
            pltpu.VMEM((256, 2048), BF16),
            pltpu.VMEM((2048, 1280), BF16),
            pltpu.VMEM((2048, 256), BF16),
            pltpu.VMEM((2048, 256), BF16),
            pltpu.VMEM((2048, 256), BF16),
            pltpu.VMEM((1280, 256), BF16),
            pltpu.VMEM((256, 256), BF16),
            pltpu.VMEM((PEERS, MSG, 128), F32),
            pltpu.VMEM((2, PEERS, MSG, 128), F32),
            pltpu.VMEM((2, 128, 128), F32),
            pltpu.VMEM((2, 2, 128, 128), F32),
            pltpu.VMEM((2, 64, 128), F32),
            pltpu.VMEM((2, 2, 64, 128), F32),
            pltpu.VMEM((2, 2, 8, 128), F32),
            pltpu.VMEM((8, 64, 128), F32),
            pltpu.VMEM((8, 64, 128), F32),
            pltpu.VMEM((8, 32, 128), F32),
            pltpu.VMEM((8, 32, 128), F32),
        ]
        + [pltpu.VMEM((ROWS, 128), F32)] * 5
        + [
            dma,
            dma((2,)),
            dma((6,)),
            dma((2, 6)),
            dma((8,)),
            dma((8,)),
            dma((8,)),
            dma((8,)),
        ],
        compiler_params=pltpu.CompilerParams(
            collective_id=0, has_side_effects=True, vmem_limit_bytes=50 * 1024 * 1024
        ),
    )(
        source.reshape(128, 256),
        storage.reshape(128, 256),
        gbf,
        gbm,
        sbf,
        sbm,
    )
    return result.reshape(source.shape)


def solution(mesh):
    in_specs = (
        P("grp", "gx", "gy", None),
        P("grp", "gx", "gy", None),
        P(("gx", "gy"), None),
        P(("gx", "gy")),
        P(("gx", "gy"), None),
        P(("gx", "gy"), None),
    )
    return jax.shard_map(
        per_device, mesh=mesh, in_specs=in_specs, out_specs=P("grp", "gx", "gy", None), check_vma=False
    )
```

time: 932 us -> 497 us (0.53); the launches traced: 917 us -> 496 us
  waiting for transfers between devices: 393 us -> 0 us
  starting transfers between devices: 370 us -> 0 us
  blocking collectives: 0 us -> 323 us
  Pallas kernels: 0 us -> 139 us
  local copies, waits for them, and re-layouts: 91.6 us -> 30.1 us
  other arithmetic: 39 us -> 4.53 us
  matrix products: 20.9 us -> 0 us
    all_gather x0 -> x1, blocking collectives: none -> 323 us  [tables(): lax.all_gather(mine, ('gx', 'gy'), axis=0, tiled=False)]
    all_to_all x34 -> x0, waiting for transfers between devices: 292 us -> none  [the longest x8 99.1 us: operate(): lax.all_to_all(send_tile, ('gx', 'gy'), split_axis=0, concat_axis=0, tile...]
    all_to_all x34 -> x0, starting transfers between devices: 271 us -> none  [the longest x8 73.8 us: operate(): lax.all_to_all(flux, ('gx', 'gy'), split_axis=0, concat_axis=0, tiled=True)]
    pallas_call x0 -> x1, Pallas kernels: none -> 139 us  [per_device(): pl.pallas_call(kernel, out_shape=jax.ShapeDtypeStruct((128, 256), F32), i...]
    ppermute x48 -> x0, waiting for transfers between devices: 101 us -> none  [the longest x16 93.9 us: swapped(): lax.ppermute(value, axis, [(i, i ^ 1 << bit) for i in range(lax.axis_size...]
    ppermute x48 -> x0, starting transfers between devices: 99 us -> none  [the longest x16 51.9 us: with_halo(): lax.ppermute(tail, axis, [(i, (i + 1) % count) for i in range(ends)])]
    gather x66 -> x0, local copies, waits for them, and re-layouts: 50.8 us -> none  [the longest x16 13.8 us: operate(): tiles[jnp.maximum(flat_target, 0)] - flat_arrived]
    select_n x45 -> x1, other arithmetic: 32.1 us -> 0.85 us  [tables(): sent = jnp.where(sent > 0, u[:, None, None] + (sent - 1) // 128, -1)]
  transfers between devices with their start and end apart: 82 -> 0, of which waited for: 50 -> 0; matrix products, arithmetic and copies ran while one was open for 12% -> 0% of each run, Pallas kernels for 0% -> 0%
where the time goes in v1:
time: 497 us; the launch traced here: 496 us
  blocking collectives  323 us (65%)
  Pallas kernels  139 us (28%)
  local copies, waits for them, and re-layouts  30.1 us (6%)
    all_gather x1, blocking collectives, tables(): lax.all_gather(mine, ('gx', 'gy'), axis=0, tiled=False)  323 us
    pallas_call x1, Pallas kernels, per_device(): pl.pallas_call(kernel, out_shape=jax.ShapeDtypeStruct((128, 256), F32), i...  139 us
    reshape x1, local copies, waits for them, and re-layouts, tables(): lax.all_gather(mine, ('gx', 'gy'), axis=0, tiled=False)  17.6 us

profile of v1, /device:TPU:3, one launch (start us, length us, event | category | flops | bytes accessed | tf_op | source)
XLA Modules:
  0.0 496.5 jit_solution(10521886078409573051)
XLA Ops:
  0.0 0.7 add_add_fusion
  0.7 0.9 convert_reduce_fusion.1
  1.6 0.7 multiply_add_fusion.1
  2.3 0.8 copy.77
  3.1 0.1 reshape.100
  3.3 0.8 copy.76
  4.1 0.1 eq.60
  4.2 0.2 convert_reduce_fusion
  4.4 0.2 select_reduce_fusion
  4.6 322.5 %all-gather.1 = s32[128,6,128]{2,1,0:T(8,128)S(1)} all-gather(s32[1,6,128]{2,1,0:T(8,128)S(1)} %add_bitcast_fusion), channel_id=2, replica_groups=mesh['grp'=2,'gx'=32,'gy'=4] {'gx','gy'}, dimensions={0}, use_global_device_ids=true | all-gather | bytes 396288 | tf_op jit(solution)/shard_map/all_gather | solution.py:445
  327.2 17.6 %reshape.103 = s32[8,4,4,6,8,4,4]{6,5,4,2,1,0,3:T(4,128)} reshape(s32[128,6,128]{2,0,1:T(8,128)S(1)} %copy.78) | data formatting | bytes 786432 | tf_op jit(solution)/shard_map/reshape | solution.py:445
  344.8 2.3 constant_dynamic-slice_fusion
  347.1 2.6 copy.96
  349.7 1.0 constant_dynamic-slice_fusion.1
  350.7 0.7 copy.79
  351.3 0.5 dynamic-slice_add_fusion
  351.9 0.9 fusion.3
  352.9 1.0 copy.86
  354.0 0.5 copy.87
  354.5 0.1 reshape_reshape.3.gbm
  355.7 0.3 copy.92
  356.0 0.3 copy.94
  356.8 139.0 %shard_map.64 = f32[128,256]{1,0:T(8,128)S(1)} custom-call(f32[128,256]{1,0:T(8,128)S(1)} %bitcast.32, f32[128,256]{1,0:T(8,128)S(1)} %bitcast.33, s32[1280,4]{1,0:T(8,128)S(1)} %bitcast.30, s32[256,4]{1,0:T(8,128)S(1)} %reshape_reshape.3.gbm, s32[4,1280]{1,0:T(4,128)S(1)} %bitcast.34, s32[4,256]{1,0:T(4,128)S(1)} %bitcast.35), custom_call_target="tpu_custom_call" | custom-call | tf_op jit(solution)/shard_map/pallas_call | solution.py:477
  495.8 0.7 copy.98
  (41 shorter events, 1.8 us)
Async XLA Ops:
  327.2 29.6 %copy-start = (f32[1,16,8,256]{3,2,1,0:T(8,128)S(1)}, f32[1,16,8,256]{3,2,1,0:T(8,128)}, u32[]{:S(2)}) copy-start(f32[1,16,8,256]{3,2,1,0:T(8,128)} %param.6) | copy-start | bytes 393220
  327.2 29.6 %copy-start.1 = (f32[1,16,8,256]{3,2,1,0:T(8,128)S(1)}, f32[1,16,8,256]{3,2,1,0:T(8,128)}, u32[]{:S(2)}) copy-start(f32[1,16,8,256]{3,2,1,0:T(8,128)} %param.7) | copy-start | bytes 393220

commit v2 on v1

--- a/solution.py
+++ b/solution.py
@@ -46,12 +46,12 @@
 
 
 def kernel(
-    src, sto, gbf, gbm, sbf, sbm, out,
+    src, sto, tab, out,
     gf, gm, sf, sm, wf, wm, rf, rm,
     send, recv, hs, hz, ys, hy, hx,
-    tx, rx, tx2, rx2,
+    tx, rx, tx2, rx2, mo, mi, vs,
     d_ref, r_ref, p_ref, c_ref, i_ref,
-    send_sem, recv_sem, hsend_sem, hrecv_sem, tsend_sem, trecv_sem, usend_sem, urecv_sem,
+    send_sem, recv_sem, hsend_sem, hrecv_sem, tsend_sem, trecv_sem, usend_sem, urecv_sem, msend_sem, mrecv_sem,
 ):
     g = lax.axis_index("grp")
     gx = lax.axis_index("gx")
@@ -106,6 +106,7 @@
                 piece = ref[q * 32:(q + 1) * 32, half * 128:(half + 1) * 128]
                 acc = jnp.where(l32 // 32 == q, turn(piece, 32 * (q - part)), acc)
             tx[z, a * 32:(a + 1) * 32, :] = acc
+        tx[z, 64:72, :] = tab[...]
 
     pl.semaphore_wait(barrier, PEERS - 1 + 2 + jnp.where(own, 14, 16))
 
@@ -134,65 +135,58 @@
 
     lax.fori_loop(0, 8, far_start, 0)
 
-    iota_cols = lax.broadcasted_iota(I32, (80, ROWS), 1)
-
-    def build_g(j, carry):
-        at = pl.multiple_of(j * 80, 80)
-        rows = gbf[pl.ds(at, 80), :]
-        for q in range(4):
-            hit = rows[:, q:q + 1] == iota_cols
-            gf[pl.ds(at, 80), q * ROWS:(q + 1) * ROWS] = jnp.where(hit, 1.0, 0.0).astype(BF16)
-        at = pl.multiple_of(j * 16, 16)
-        rows = gbm[pl.ds(at, 16), :]
-        for q in range(4):
-            hit = rows[:, q:q + 1] == iota_cols[:16]
-            gm[pl.ds(at, 16), q * ROWS:(q + 1) * ROWS] = jnp.where(hit, 1.0, 0.0).astype(BF16)
-        return carry
-
-    lax.fori_loop(0, 16, build_g, 0)
-
-    within = lax.broadcasted_iota(I32, (1, 1280), 1) % 40
-    weight = jnp.where(within < 32, TI, TM)
-
-    def build_s(j, carry):
-        at = pl.multiple_of(j * 16, 16)
-        block = lax.broadcasted_iota(I32, (16, 1280), 0) + at
-        for q in range(4):
-            sf[pl.ds(at + q * ROWS, 16), :] = jnp.where(sbf[q:q + 1, :] == block, weight, 0.0).astype(BF16)
-            sm[pl.ds(at + q * ROWS, 16), :] = jnp.where(
-                sbm[q:q + 1, :] == block[:, :256], TM, 0.0
-            ).astype(BF16)
-        return carry
-
-    lax.fori_loop(0, 32, build_s, 0)
+    def far_wait(n, carry):
+        mine = own & (n == g * 4 + u_home)
+
+        @pl.when(jnp.logical_not(mine))
+        def _():
+            pltpu.make_async_copy(rx.at[n], rx.at[n], trecv_sem.at[n]).wait()
+
+        @pl.when(jnp.logical_not(own & (n == cz)))
+        def _():
+            pltpu.make_async_copy(tx.at[n], tx.at[n], tsend_sem.at[n]).wait()
+
+        return carry
+
+    lax.fori_loop(0, 8, far_wait, 0)
+
+    lane1 = lax.broadcasted_iota(I32, (1, 128), 1)
+    ub1 = lane1 // 32
+    ua1 = lane1 % 32 // 8
+    t1 = lane1 % 8
+    k32 = lax.broadcasted_iota(I32, (32, 128), 0)
+    table = rx[0:4, 64:72, :].reshape(32, 128)
+    table = jnp.concatenate([table] * 4, axis=0)
+    first_of = ((w + k32 // 4) % 8) * 16 + (gy + k32 % 4) % 4
+    outgoing = jnp.zeros((32, 128), F32)
+    for ub in range(4):
+        chosen = jnp.where(first_of + ub * 4 == l32, 1.0, 0.0)
+        x = lax.dot_general(
+            chosen, table, (((1,), (1,)), ((), ())),
+            precision=lax.Precision.HIGHEST, preferred_element_type=F32,
+        )
+        outgoing = jnp.where(ub1 == ub, x, outgoing)
+    mo[...] = jnp.broadcast_to(outgoing[:, None, :], (32, 8, 128)).reshape(256, 128)
+    mi[0:8] = mo[0:8]
+
+    def edge_send(k, carry):
+        at = pl.multiple_of(k * 8, 8)
+        pltpu.make_async_remote_copy(
+            src_ref=mo.at[pl.ds(at, 8)],
+            dst_ref=mi.at[pl.ds(at, 8)],
+            send_sem=msend_sem,
+            recv_sem=mrecv_sem,
+            device_id=peer(k),
+            device_id_type=MESH,
+        ).start()
+        return carry
+
+    lax.fori_loop(1, PEERS, edge_send, 0)
 
     ln = lanes(ROWS)
     group = ln // 32
     is_f = ln < 32
     is_m = group == 1
-
-    entering = jnp.where(lax.broadcasted_iota(I32, (1280, 128), 0) % 40 < 16, 1.0, 0.0).astype(BF16)
-    ones = jnp.ones((256, 128), BF16)
-    indeg = jnp.zeros((ROWS, 128), F32)
-    hosted = jnp.zeros((ROWS, 128), F32)
-    for q in range(4):
-        indeg = indeg + jnp.dot(sf[q * ROWS:(q + 1) * ROWS, :], entering, preferred_element_type=F32)
-        hosted = hosted + jnp.dot(sm[q * ROWS:(q + 1) * ROWS, :], ones, preferred_element_type=F32)
-
-    def far_wait(n, carry):
-        mine = own & (n == g * 4 + u_home)
-
-        @pl.when(jnp.logical_not(mine))
-        def _():
-            pltpu.make_async_copy(rx.at[n], rx.at[n], trecv_sem.at[n]).wait()
-
-        @pl.when(jnp.logical_not(own & (n == cz)))
-        def _():
-            pltpu.make_async_copy(tx.at[n], tx.at[n], tsend_sem.at[n]).wait()
-
-        return carry
-
-    lax.fori_loop(0, 8, far_wait, 0)
 
     pairs, theta = coefficients()
     for a, ref in ((0, r_ref), (1, c_ref)):
@@ -208,9 +202,116 @@
     stored = c_ref[...]
     inverse = 1.0 / (stored + jnp.where(is_f, 4.0 * TF + 4.0 * TI + TM, 6.0 + TM))
     i_ref[...] = inverse
-    c_ref[...] = stored + jnp.where(is_f, 4.0 * TF + 2.0 * TI + TM + indeg, 6.0 + hosted)
+    c_ref[...] = stored
     d_ref[...] = r_ref[...] * inverse * (1.0 / theta)
     p_ref[...] = jnp.zeros((ROWS, 128), F32)
+
+    pltpu.make_async_copy(mi.at[pl.ds(8, 248)], mi.at[pl.ds(8, 248)], mrecv_sem).wait()
+    incoming = mi[pl.ds(0, 32, stride=8), :]
+    mirror = ((8 - k32 // 4) % 8) * 4 + (4 - k32 % 4) % 4
+    mirror = jnp.where(mirror == l32, 1.0, 0.0)[:, :32]
+
+    def mirrored(x):
+        return jnp.dot(mirror, x, precision=lax.Precision.HIGHEST, preferred_element_type=F32)
+
+    def source_row(x):
+        x = x.astype(I32)
+        return jnp.where(x > 0, ua1 * 128 + ((x - 1) >> 7) + 1, 0)
+
+    def target_row(x):
+        x = x.astype(I32)
+        return jnp.where(x > 0, ub1 * 128 + ((x - 1) & 127) + 1, 0)
+
+    vs[0] = source_row(outgoing)
+    vs[1] = target_row(mirrored(incoming))
+    vs[2] = target_row(incoming)
+    vs[3] = source_row(mirrored(outgoing))
+
+    inter_at = jnp.where(t1 < 4, ua1 * 4 + ub1, -100)
+    host_at = jnp.where((t1 == 4) | (t1 == 5), ua1 * 2 + t1 - 4, -100)
+    out_at = jnp.maximum(inter_at + 8, host_at)
+    back_at = jnp.maximum(inter_at + 16, host_at + 32)
+    i80 = lax.broadcasted_iota(I32, (80, 128), 0)
+    first80 = i80 < 40
+    i80 = i80 % 40
+    i16 = lax.broadcasted_iota(I32, (16, 128), 0)
+    first16 = i16 < 8
+    i16 = i16 % 8
+    ql = lax.broadcasted_iota(I32, (256, 512), 0)
+    qt = ql % 8
+    qh = jnp.where(qt < 4, qt, (ql % 128) // 32)
+    q_rep = jnp.where(
+        lax.broadcasted_iota(I32, (256, 512), 1) // 128 == qh, jnp.where(ql < 128, 32.0, 1.0), 0.0
+    ).astype(BF16)
+    ql = lax.broadcasted_iota(I32, (16, 256), 1)
+    qt = ql % 8
+    qh = jnp.where(qt < 4, qt, (ql % 128) // 32)
+    q_row = jnp.where(
+        lax.broadcasted_iota(I32, (16, 256), 0) == qh, jnp.where(ql < 128, 32.0, 1.0), 0.0
+    ).astype(BF16)
+
+    def halves(x):
+        return jnp.concatenate([(x >> 5).astype(F32), (x & 31).astype(F32)], axis=1).astype(BF16)
+
+    def build_g(j, carry):
+        def pair(n, first):
+            return jnp.where(first, vs[n, pl.ds(2 * j, 1), :], vs[n, pl.ds(2 * j + 1, 1), :])
+
+        at = pl.multiple_of(j * 80, 80)
+        x = jnp.where(i80 == out_at, pair(0, first80), 0)
+        x = x + jnp.where(i80 == inter_at + 24, pair(1, first80), 0)
+        rows = jnp.dot(halves(x), q_rep, preferred_element_type=F32).astype(I32)
+        for q in range(4):
+            for c in range(4):
+                hit = rows[:, q * 128:(q + 1) * 128] == lane1 + (c * 128 + 1)
+                gf[pl.ds(at, 80), q * ROWS + c * 128:q * ROWS + (c + 1) * 128] = jnp.where(
+                    hit, 1.0, 0.0
+                ).astype(BF16)
+        x = jnp.where(i80 == inter_at, pair(2, first80), 0)
+        x = x + jnp.where(i80 == back_at, pair(3, first80), 0)
+        rf[pl.ds(at, 80), :] = halves(x)
+        at = pl.multiple_of(j * 16, 16)
+        x = jnp.where(i16 == host_at, pair(1, first16), 0)
+        rows = jnp.dot(halves(x), q_rep, preferred_element_type=F32).astype(I32)
+        for q in range(4):
+            for c in range(4):
+                hit = rows[:, q * 128:(q + 1) * 128] == lane1 + (c * 128 + 1)
+                gm[pl.ds(at, 16), q * ROWS + c * 128:q * ROWS + (c + 1) * 128] = jnp.where(
+                    hit, 1.0, 0.0
+                ).astype(BF16)
+        rm[pl.ds(at, 16), :] = halves(jnp.where(i16 == host_at, pair(2, first16), 0))
+        return carry
+
+    lax.fori_loop(0, 16, build_g, 0)
+
+    across = (((1,), (1,)), ((), ()))
+    sbf = lax.dot_general(q_row, rf[...], across, preferred_element_type=F32).astype(I32)
+    sbm = lax.dot_general(q_row, rm[...], across, preferred_element_type=F32).astype(I32)
+    within = lax.broadcasted_iota(I32, (1, 1280), 1) % 40
+    weight = jnp.where(within < 32, TI, TM)
+
+    def build_s(j, carry):
+        at = pl.multiple_of(j * 16, 16)
+        block = lax.broadcasted_iota(I32, (16, 1280), 0) + (at + 1)
+        for q in range(4):
+            sf[pl.ds(at + q * ROWS, 16), :] = jnp.where(sbf[q:q + 1, :] == block, weight, 0.0).astype(BF16)
+            sm[pl.ds(at + q * ROWS, 16), :] = jnp.where(
+                sbm[q:q + 1, :] == block[:, :256], TM, 0.0
+            ).astype(BF16)
+        return carry
+
+    lax.fori_loop(0, 32, build_s, 0)
+
+    entering = jnp.where(lax.broadcasted_iota(I32, (1280, 128), 0) % 40 < 16, 1.0, 0.0).astype(BF16)
+    ones = jnp.ones((256, 128), BF16)
+    indeg = jnp.zeros((ROWS, 128), F32)
+    hosted = jnp.zeros((ROWS, 128), F32)
+    for q in range(4):
+        indeg = indeg + jnp.dot(sf[q * ROWS:(q + 1) * ROWS, :], entering, preferred_element_type=F32)
+        hosted = hosted + jnp.dot(sm[q * ROWS:(q + 1) * ROWS, :], ones, preferred_element_type=F32)
+
+    c_ref[...] = c_ref[...] + jnp.where(is_f, 4.0 * TF + 2.0 * TI + TM + indeg, 6.0 + hosted)
+    pltpu.make_async_copy(mo.at[pl.ds(8, 248)], mo.at[pl.ds(8, 248)], msend_sem).wait()
 
     low = jnp.where(cz > 0, 1.0, 0.0)
     high = jnp.where(cz < 7, 1.0, 0.0)
@@ -430,54 +531,20 @@
     return jnp.sum(jnp.where(key[None, :] == wanted[:, None], code[None, :], 0), axis=1).reshape(most, 128)
 
 
-def tables(host_device, host_column, inter_device, inter_slot):
-    g = lax.axis_index("grp")
-    gx = lax.axis_index("gx")
-    gy = lax.axis_index("gy")
-    w = (gx // 16) * 4 + g * 2 + gx % 2
-    mine = jnp.concatenate(
+def per_device(source, storage, host_device, host_column, inter_device, inter_slot):
+    table = jnp.concatenate(
         [
             edge_table(inter_device.reshape(-1), inter_slot.reshape(-1), 2, 4),
             edge_table(host_device.reshape(-1), host_column, 1, 2),
+            jnp.zeros((2, 128), I32),
         ],
         axis=0,
-    )
-    every = lax.all_gather(mine, ("gx", "gy"), axis=0, tiled=False).reshape(8, 4, 4, 6, 8, 4, 4)
-    sent = lax.dynamic_slice(every, (w, 0, gy, 0, 0, 0, 0), (1, 4, 1, 6, 8, 4, 4)).reshape(4, 6, 8, 4, 4)
-    came = lax.dynamic_slice(every, (0, 0, 0, 0, w, 0, gy), (8, 4, 4, 6, 1, 4, 1)).reshape(8, 4, 4, 6, 4)
-
-    def relative(x):
-        x = lax.dynamic_slice_in_dim(jnp.concatenate([x, x], axis=0), w, 8, axis=0)
-        return lax.dynamic_slice_in_dim(jnp.concatenate([x, x], axis=1), gy, 4, axis=1)
-
-    sent = relative(sent.transpose(2, 4, 0, 3, 1))
-    came = relative(came.transpose(0, 2, 1, 4, 3))
-    u = jnp.arange(4, dtype=I32) * 128
-    sent = jnp.where(sent > 0, u[:, None, None] + (sent - 1) // 128, -1)
-    came = jnp.where(came > 0, u[None, :, None] + (came - 1) % 128, -1)
-    f_out = sent[..., :4].reshape(8, 4, 16, 4)
-    h_out = sent[..., 4:].reshape(8, 4, 8, 4)
-    f_in = came[..., :4].reshape(8, 4, 16, 4)
-    h_in = came[..., 4:].reshape(8, 4, 8, 4)
-
-    def mirror(x):
-        x = jnp.concatenate([x[:1], x[:0:-1]], axis=0)
-        return jnp.concatenate([x[:, :1], x[:, :0:-1]], axis=1)
-
-    gbf = jnp.concatenate([h_out, f_out, f_in], axis=2).reshape(1280, 4)
-    gbm = h_in.reshape(256, 4)
-    sbf = mirror(jnp.concatenate([f_in, f_out, h_out], axis=2)).reshape(1280, 4).T
-    sbm = mirror(h_in).reshape(256, 4).T
-    return gbf, gbm, sbf, sbm
-
-
-def per_device(source, storage, host_device, host_column, inter_device, inter_slot):
-    gbf, gbm, sbf, sbm = tables(host_device, host_column, inter_device, inter_slot)
+    ).astype(F32)
     dma = pltpu.SemaphoreType.DMA
     result = pl.pallas_call(
         kernel,
         out_shape=jax.ShapeDtypeStruct((128, 256), F32),
-        in_specs=[pl.BlockSpec(memory_space=pltpu.VMEM)] * 6,
+        in_specs=[pl.BlockSpec(memory_space=pltpu.VMEM)] * 3,
         out_specs=pl.BlockSpec(memory_space=pltpu.VMEM),
         scratch_shapes=[
             pltpu.VMEM((1280, 2048), BF16),
@@ -495,10 +562,13 @@
             pltpu.VMEM((2, 64, 128), F32),
             pltpu.VMEM((2, 2, 64, 128), F32),
             pltpu.VMEM((2, 2, 8, 128), F32),
-            pltpu.VMEM((8, 64, 128), F32),
-            pltpu.VMEM((8, 64, 128), F32),
+            pltpu.VMEM((8, 72, 128), F32),
+            pltpu.VMEM((8, 72, 128), F32),
             pltpu.VMEM((8, 32, 128), F32),
             pltpu.VMEM((8, 32, 128), F32),
+            pltpu.VMEM((256, 128), F32),
+            pltpu.VMEM((256, 128), F32),
+            pltpu.VMEM((4, 32, 128), I32),
         ]
         + [pltpu.VMEM((ROWS, 128), F32)] * 5
         + [
@@ -510,6 +580,8 @@
             dma((8,)),
             dma((8,)),
             dma((8,)),
+            dma,
+            dma,
         ],
         compiler_params=pltpu.CompilerParams(
             collective_id=0, has_side_effects=True, vmem_limit_bytes=50 * 1024 * 1024
@@ -517,10 +589,7 @@
     )(
         source.reshape(128, 256),
         storage.reshape(128, 256),
-        gbf,
-        gbm,
-        sbf,
-        sbm,
+        table,
     )
     return result.reshape(source.shape)
 

time: 497 us -> 157 us (0.32)
  blocking collectives: 323 us -> 0 us
  local copies, waits for them, and re-layouts: 30.1 us -> 3.17 us
  Pallas kernels: 139 us -> 153 us
    all_gather x1 -> x0, blocking collectives: 323 us -> none  [tables(): lax.all_gather(mine, ('gx', 'gy'), axis=0, tiled=False)]
    reshape x9 -> x1, local copies, waits for them, and re-layouts: 20.8 us -> 0.14 us  [per_device(): inter_slot.reshape(-1)]
    pallas_call x1, Pallas kernels: 139 us -> 153 us  [per_device(): pl.pallas_call(kernel, out_shape=jax.ShapeDtypeStruct((128, 256), F32), i...]
where the time goes in v2:
time: 157 us
  Pallas kernels  153 us (97%)
  local copies, waits for them, and re-layouts  3.17 us (2%)
    pallas_call x1, Pallas kernels, per_device(): pl.pallas_call(kernel, out_shape=jax.ShapeDtypeStruct((128, 256), F32), i...  153 us

profile of v2, /device:TPU:3, one launch (start us, length us, event | category | flops | bytes accessed | tf_op | source)
XLA Modules:
  0.0 156.9 jit_solution(15796331200715966714)
XLA Ops:
  0.0 0.0 copy-start.5
  0.0 0.7 copy-done.5
  0.7 0.2 convert_reduce_fusion.1
  0.8 0.0 copy-start.4
  0.9 0.1 pad.2.clone
  0.9 0.6 copy-done.4
  1.5 0.1 select_reduce_fusion.1
  1.6 0.0 copy-start.2
  1.6 0.0 copy-start.3
  1.6 0.7 copy-done.2
  2.3 0.0 copy-start
  2.3 0.0 copy-start.1
  2.3 0.1 copy.9
  2.4 0.1 eq.56
  2.6 0.2 convert_reduce_fusion
  2.7 0.0 copy-done.3
  2.8 0.1 copy.10
  2.9 0.1 reshape.62
  3.0 0.1 select_reduce_fusion
  3.2 0.1 add_convert_fusion.tab
  3.2 0.0 copy-done
  3.2 0.0 copy-done.1
  3.3 153.0 %shard_map.64 = f32[128,256]{1,0:T(8,128)S(1)} custom-call(f32[128,256]{1,0:T(8,128)S(1)} %bitcast.8, f32[128,256]{1,0:T(8,128)S(1)} %bitcast.9, f32[8,128]{1,0:T(8,128)S(1)} %add_convert_fusion.tab), custom_call_target="tpu_custom_call" | custom-call | tf_op jit(solution)/shard_map/pallas_call | solution.py:544
  156.3 0.7 copy.12
  (3 shorter events, 0.0 us)
Async XLA Ops:
  0.0 0.7 copy-start.5
  0.8 0.7 copy-start.4
  1.6 0.7 copy-start.2
  1.6 1.1 copy-start.3
  2.3 0.9 copy-start
  2.3 1.0 copy-start.1

commit v3 on v2

--- a/solution.py
+++ b/solution.py
@@ -46,12 +46,12 @@
 
 
 def kernel(
-    src, sto, tab, out,
+    src, sto, host_dev, host_col, inter_dev, inter_slot, out,
     gf, gm, sf, sm, wf, wm, rf, rm,
     send, recv, hs, hz, ys, hy, hx,
-    tx, rx, tx2, rx2, mo, mi, vs,
+    tx, rx, tx2, rx2, mo, mi, vs, et, er,
     d_ref, r_ref, p_ref, c_ref, i_ref,
-    send_sem, recv_sem, hsend_sem, hrecv_sem, tsend_sem, trecv_sem, usend_sem, urecv_sem, msend_sem, mrecv_sem,
+    send_sem, recv_sem, hsend_sem, hrecv_sem, tsend_sem, trecv_sem, usend_sem, urecv_sem, msend_sem, mrecv_sem, esend_sem, erecv_sem,
 ):
     g = lax.axis_index("grp")
     gx = lax.axis_index("gx")
@@ -65,7 +65,7 @@
         return ((w_ // 2) % 2, (w_ // 4) * 16 + z_ * 2 + w_ % 2, y_)
 
     def peer(k):
-        return place((w + k // 4) % 8, (gy + k % 4) % 4, cz)
+        return place((w + k % 8) % 8, (gy + k // 8 + k % 8) % 4, cz)
 
     w_home = gx // 4
     u_home = gx % 4
@@ -96,6 +96,35 @@
         return carry
 
     lax.fori_loop(0, 8, greet_far, 0)
+
+    l128 = lanes(128)
+    s128 = lax.broadcasted_iota(I32, (128, 128), 0)
+    earlier = jnp.where(l128 < s128, 1.0, 0.0).astype(BF16)
+
+    def column(row):
+        return jnp.sum(jnp.where(l128 == s128, row.astype(F32), 0.0), axis=1, keepdims=True)
+
+    edges = jnp.zeros((8, 128), F32)
+    s8 = lax.broadcasted_iota(I32, (8, 128), 0)
+
+    def list_edges(edges, devices, rows, base, most):
+        before = jnp.zeros((1, 128), F32)
+        for dev, row in zip(devices, rows):
+            named = column(dev) == l128.astype(F32)
+            hit = jnp.where(named, 1.0, 0.0)
+            rank = before + jnp.dot(earlier, hit.astype(BF16), preferred_element_type=F32)
+            before = before + jnp.sum(hit, axis=0, keepdims=True)
+            code = jnp.where(named, column(row) + (1 + 128 * s128).astype(F32), 0.0)
+            for r in range(most):
+                x = jnp.sum(jnp.where(rank == float(r), code, 0.0), axis=0, keepdims=True)
+                edges = edges + jnp.where(s8 == base + r, x, 0.0)
+        return edges
+
+    edges = list_edges(
+        edges, [inter_dev[0:1, :], inter_dev[1:2, :]], [inter_slot[0:1, :], inter_slot[1:2, :]], 0, 4
+    )
+    edges = list_edges(edges, [host_dev[...]], [host_col[...]], 4, 2)
+    et[...] = edges
 
     l32 = lanes(32)
     for z in range(8):
@@ -106,9 +135,32 @@
                 piece = ref[q * 32:(q + 1) * 32, half * 128:(half + 1) * 128]
                 acc = jnp.where(l32 // 32 == q, turn(piece, 32 * (q - part)), acc)
             tx[z, a * 32:(a + 1) * 32, :] = acc
-        tx[z, 64:72, :] = tab[...]
 
     pl.semaphore_wait(barrier, PEERS - 1 + 2 + jnp.where(own, 14, 16))
+
+    def edge_start(z, carry):
+        mine = own & (z == cz)
+
+        @pl.when(mine)
+        def _():
+            er[u_home] = et[...]
+
+        @pl.when(jnp.logical_not(mine))
+        def _():
+            pltpu.make_async_remote_copy(
+                src_ref=et,
+                dst_ref=er.at[u_home],
+                send_sem=esend_sem.at[z],
+                recv_sem=erecv_sem.at[u_home],
+                device_id=place(w_home, gy, z),
+                device_id_type=MESH,
+            ).start()
+
+        return carry
+
+    @pl.when(g == 0)
+    def _():
+        lax.fori_loop(0, 8, edge_start, 0)
 
     def far_copy(z):
         return pltpu.make_async_remote_copy(
@@ -135,29 +187,23 @@
 
     lax.fori_loop(0, 8, far_start, 0)
 
-    def far_wait(n, carry):
-        mine = own & (n == g * 4 + u_home)
-
-        @pl.when(jnp.logical_not(mine))
-        def _():
-            pltpu.make_async_copy(rx.at[n], rx.at[n], trecv_sem.at[n]).wait()
-
-        @pl.when(jnp.logical_not(own & (n == cz)))
-        def _():
-            pltpu.make_async_copy(tx.at[n], tx.at[n], tsend_sem.at[n]).wait()
-
-        return carry
-
-    lax.fori_loop(0, 8, far_wait, 0)
+    def edge_wait(n, carry):
+        @pl.when(jnp.logical_not(own & (g == 0) & (n == u_home)))
+        def _():
+            pltpu.make_async_copy(er.at[n], er.at[n], erecv_sem.at[n]).wait()
+
+        return carry
+
+    lax.fori_loop(0, 4, edge_wait, 0)
 
     lane1 = lax.broadcasted_iota(I32, (1, 128), 1)
     ub1 = lane1 // 32
     ua1 = lane1 % 32 // 8
     t1 = lane1 % 8
     k32 = lax.broadcasted_iota(I32, (32, 128), 0)
-    table = rx[0:4, 64:72, :].reshape(32, 128)
+    table = er[...].reshape(32, 128)
     table = jnp.concatenate([table] * 4, axis=0)
-    first_of = ((w + k32 // 4) % 8) * 16 + (gy + k32 % 4) % 4
+    first_of = ((w + k32 % 8) % 8) * 16 + (gy + k32 // 8 + k32 % 8) % 4
     outgoing = jnp.zeros((32, 128), F32)
     for ub in range(4):
         chosen = jnp.where(first_of + ub * 4 == l32, 1.0, 0.0)
@@ -183,32 +229,10 @@
 
     lax.fori_loop(1, PEERS, edge_send, 0)
 
-    ln = lanes(ROWS)
-    group = ln // 32
-    is_f = ln < 32
-    is_m = group == 1
-
-    pairs, theta = coefficients()
-    for a, ref in ((0, r_ref), (1, c_ref)):
-        for u in range(4):
-            fr = rx[4 + u, a * 32:(a + 1) * 32, :]
-            ma = rx[u, a * 32:(a + 1) * 32, :]
-            for q in range(4):
-                ref[u * 128 + q * 32:u * 128 + (q + 1) * 32, :] = jnp.where(
-                    l32 < 32,
-                    turn(fr, -32 * q),
-                    jnp.where(l32 // 32 == 1, turn(ma, 32 - 32 * q), 0.0),
-                )
-    stored = c_ref[...]
-    inverse = 1.0 / (stored + jnp.where(is_f, 4.0 * TF + 4.0 * TI + TM, 6.0 + TM))
-    i_ref[...] = inverse
-    c_ref[...] = stored
-    d_ref[...] = r_ref[...] * inverse * (1.0 / theta)
-    p_ref[...] = jnp.zeros((ROWS, 128), F32)
-
     pltpu.make_async_copy(mi.at[pl.ds(8, 248)], mi.at[pl.ds(8, 248)], mrecv_sem).wait()
     incoming = mi[pl.ds(0, 32, stride=8), :]
-    mirror = ((8 - k32 // 4) % 8) * 4 + (4 - k32 % 4) % 4
+    mirror_w = (8 - k32 % 8) % 8
+    mirror = mirror_w + 8 * ((16 - k32 // 8 - k32 % 8 - mirror_w) % 4)
     mirror = jnp.where(mirror == l32, 1.0, 0.0)[:, :32]
 
     def mirrored(x):
@@ -302,6 +326,44 @@
 
     lax.fori_loop(0, 32, build_s, 0)
 
+    def far_wait(n, carry):
+        mine = own & (n == g * 4 + u_home)
+
+        @pl.when(jnp.logical_not(mine))
+        def _():
+            pltpu.make_async_copy(rx.at[n], rx.at[n], trecv_sem.at[n]).wait()
+
+        @pl.when(jnp.logical_not(own & (n == cz)))
+        def _():
+            pltpu.make_async_copy(tx.at[n], tx.at[n], tsend_sem.at[n]).wait()
+
+        return carry
+
+    lax.fori_loop(0, 8, far_wait, 0)
+
+    ln = lanes(ROWS)
+    group = ln // 32
+    is_f = ln < 32
+    is_m = group == 1
+
+    pairs, theta = coefficients()
+    for a, ref in ((0, r_ref), (1, c_ref)):
+        for u in range(4):
+            fr = rx[4 + u, a * 32:(a + 1) * 32, :]
+            ma = rx[u, a * 32:(a + 1) * 32, :]
+            for q in range(4):
+                ref[u * 128 + q * 32:u * 128 + (q + 1) * 32, :] = jnp.where(
+                    l32 < 32,
+                    turn(fr, -32 * q),
+                    jnp.where(l32 // 32 == 1, turn(ma, 32 - 32 * q), 0.0),
+                )
+    stored = c_ref[...]
+    inverse = 1.0 / (stored + jnp.where(is_f, 4.0 * TF + 4.0 * TI + TM, 6.0 + TM))
+    i_ref[...] = inverse
+    c_ref[...] = stored
+    d_ref[...] = r_ref[...] * inverse * (1.0 / theta)
+    p_ref[...] = jnp.zeros((ROWS, 128), F32)
+
     entering = jnp.where(lax.broadcasted_iota(I32, (1280, 128), 0) % 40 < 16, 1.0, 0.0).astype(BF16)
     ones = jnp.ones((256, 128), BF16)
     indeg = jnp.zeros((ROWS, 128), F32)
@@ -313,14 +375,23 @@
     c_ref[...] = c_ref[...] + jnp.where(is_f, 4.0 * TF + 2.0 * TI + TM + indeg, 6.0 + hosted)
     pltpu.make_async_copy(mo.at[pl.ds(8, 248)], mo.at[pl.ds(8, 248)], msend_sem).wait()
 
+    def edge_sent(z, carry):
+        @pl.when(jnp.logical_not(own & (z == cz)))
+        def _():
+            pltpu.make_async_copy(et, et, esend_sem.at[z]).wait()
+
+        return carry
+
+    @pl.when(g == 0)
+    def _():
+        lax.fori_loop(0, 8, edge_sent, 0)
+
     low = jnp.where(cz > 0, 1.0, 0.0)
     high = jnp.where(cz < 7, 1.0, 0.0)
     left = jnp.where(w > 0, 1.0, 0.0)
     right = jnp.where(w < 7, 1.0, 0.0)
     near = jnp.where(gy > 0, 1.0, 0.0)
     beyond = jnp.where(gy < 3, 1.0, 0.0)
-    l128 = lanes(128)
-
     def packed(x):
         acc = x[0:128]
         for q in range(1, 4):
@@ -364,40 +435,37 @@
                     group == q, x, 0.0
                 ).astype(BF16)
 
-        def message(k):
+        def message(k, half):
             return pltpu.make_async_remote_copy(
                 src_ref=send.at[k],
                 dst_ref=recv.at[par, k],
                 send_sem=send_sem,
-                recv_sem=recv_sem.at[par],
+                recv_sem=recv_sem.at[par, half],
                 device_id=peer(k),
                 device_id_type=MESH,
             )
 
         def gather(c, carry):
-            at = pl.multiple_of(c * 320, 320)
+            at = c * 320 if isinstance(c, int) else pl.multiple_of(c * 320, 320)
             x = jnp.dot(gf[pl.ds(at, 320), :], wf[...], preferred_element_type=F32)
             send[pl.ds(c * 8, 8), 0:40, :] = (x[:, :128] + x[:, 128:]).reshape(8, 40, 128)
-            at = pl.multiple_of(c * 64, 64)
+            at = c * 64 if isinstance(c, int) else pl.multiple_of(c * 64, 64)
             x = jnp.dot(gm[pl.ds(at, 64), :], wm[...], preferred_element_type=F32)
             send[pl.ds(c * 8, 8), 40:48, :] = (x[:, :128] + x[:, 128:]).reshape(8, 8, 128)
             for n in range(8):
                 k = c * 8 + n
-                if n == 0:
-                    @pl.when(c > 0)
-                    def _():
-                        message(k).start()
-                else:
-                    message(k).start()
+                if n > 0 or not isinstance(c, int):
+                    message(k, c // 2).start()
             return carry
 
+        gather(0, 0)
         hs[0] = packed(jnp.where(ln < 16, turn(d, -16), turn(d, -47)))
         hs[1] = packed(jnp.where(ln < 16, d, turn(d, -16)))
         ys[0] = d_ref[pl.ds(0, 64, stride=8), :]
         ys[1] = d_ref[pl.ds(7, 64, stride=8), :]
         for copy in halos:
             copy.start()
-        lax.fori_loop(0, 4, gather, 0)
+        lax.fori_loop(1, 4, gather, 0)
         recv[par, 0] = send[0]
 
         col = ln % 16
@@ -428,24 +496,36 @@
         p_ref[...] = p_ref[...] + d
         r_ref[...] = r_ref[...] - (c_ref[...] * d - nb)
 
-        pltpu.make_async_copy(
-            recv.at[par, pl.ds(1, PEERS - 1)], recv.at[par, pl.ds(1, PEERS - 1)], recv_sem.at[par]
-        ).wait()
-        x = recv[par, :, 8:48, :].reshape(1280, 128)
-        hi = x.astype(BF16)
-        rf[:, 0:128] = hi
-        rf[:, 128:256] = (x - hi.astype(F32)).astype(BF16)
-        x = recv[par, :, 0:8, :].reshape(256, 128)
-        hi = x.astype(BF16)
-        rm[:, 0:128] = hi
-        rm[:, 128:256] = (x - hi.astype(F32)).astype(BF16)
         sum_f = jnp.zeros((ROWS, 128), F32)
         sum_m = jnp.zeros((ROWS, 128), F32)
-        for q in range(4):
-            x = jnp.dot(sf[q * ROWS:(q + 1) * ROWS, :], rf[...], preferred_element_type=F32)
-            sum_f = jnp.where(group == q, x[:, :128] + x[:, 128:], sum_f)
-            x = jnp.dot(sm[q * ROWS:(q + 1) * ROWS, :], rm[...], preferred_element_type=F32)
-            sum_m = jnp.where(group == q, x[:, :128] + x[:, 128:], sum_m)
+        for half in range(2):
+            came = recv.at[par, pl.ds(1, 15)] if half == 0 else recv.at[par, pl.ds(16, 16)]
+            pltpu.make_async_copy(came, came, recv_sem.at[par, half]).wait()
+            x = recv[par, half * 16:(half + 1) * 16, 8:48, :].reshape(640, 128)
+            hi = x.astype(BF16)
+            rf[half * 640:(half + 1) * 640, 0:128] = hi
+            rf[half * 640:(half + 1) * 640, 128:256] = (x - hi.astype(F32)).astype(BF16)
+            x = recv[par, half * 16:(half + 1) * 16, 0:8, :].reshape(128, 128)
+            hi = x.astype(BF16)
+            rm[half * 128:(half + 1) * 128, 0:128] = hi
+            rm[half * 128:(half + 1) * 128, 128:256] = (x - hi.astype(F32)).astype(BF16)
+            add_f = jnp.zeros((ROWS, 128), F32)
+            add_m = jnp.zeros((ROWS, 128), F32)
+            for q in range(4):
+                x = jnp.dot(
+                    sf[q * ROWS:(q + 1) * ROWS, half * 640:(half + 1) * 640],
+                    rf[half * 640:(half + 1) * 640, :],
+                    preferred_element_type=F32,
+                )
+                add_f = jnp.where(group == q, x[:, :128] + x[:, 128:], add_f)
+                x = jnp.dot(
+                    sm[q * ROWS:(q + 1) * ROWS, half * 128:(half + 1) * 128],
+                    rm[half * 128:(half + 1) * 128, :],
+                    preferred_element_type=F32,
+                )
+                add_m = jnp.where(group == q, x[:, :128] + x[:, 128:], add_m)
+            sum_f = sum_f + add_f
+            sum_m = sum_m + add_m
         sum_f = sum_f + turn(sum_f, 64)
         sum_f = sum_f + turn(sum_f, 32)
         sum_m = sum_m + turn(sum_m, 64)
@@ -520,31 +600,12 @@
             out[q * 32:(q + 1) * 32, half * 128:(half + 1) * 128] = acc
 
 
-def edge_table(dest, where_to, per_row, most):
-    count = dest.shape[0]
-    order = jnp.arange(count, dtype=I32)
-    same = (dest[:, None] == dest[None, :]) & (order[None, :] < order[:, None])
-    rank = jnp.sum(same.astype(I32), axis=1)
-    code = 1 + (order // per_row) * 128 + where_to
-    key = rank * 128 + dest
-    wanted = jnp.arange(most * 128, dtype=I32)
-    return jnp.sum(jnp.where(key[None, :] == wanted[:, None], code[None, :], 0), axis=1).reshape(most, 128)
-
-
 def per_device(source, storage, host_device, host_column, inter_device, inter_slot):
-    table = jnp.concatenate(
-        [
-            edge_table(inter_device.reshape(-1), inter_slot.reshape(-1), 2, 4),
-            edge_table(host_device.reshape(-1), host_column, 1, 2),
-            jnp.zeros((2, 128), I32),
-        ],
-        axis=0,
-    ).astype(F32)
     dma = pltpu.SemaphoreType.DMA
     result = pl.pallas_call(
         kernel,
         out_shape=jax.ShapeDtypeStruct((128, 256), F32),
-        in_specs=[pl.BlockSpec(memory_space=pltpu.VMEM)] * 3,
+        in_specs=[pl.BlockSpec(memory_space=pltpu.VMEM)] * 6,
         out_specs=pl.BlockSpec(memory_space=pltpu.VMEM),
         scratch_shapes=[
             pltpu.VMEM((1280, 2048), BF16),
@@ -562,18 +623,20 @@
             pltpu.VMEM((2, 64, 128), F32),
             pltpu.VMEM((2, 2, 64, 128), F32),
             pltpu.VMEM((2, 2, 8, 128), F32),
-            pltpu.VMEM((8, 72, 128), F32),
-            pltpu.VMEM((8, 72, 128), F32),
+            pltpu.VMEM((8, 64, 128), F32),
+            pltpu.VMEM((8, 64, 128), F32),
             pltpu.VMEM((8, 32, 128), F32),
             pltpu.VMEM((8, 32, 128), F32),
             pltpu.VMEM((256, 128), F32),
             pltpu.VMEM((256, 128), F32),
             pltpu.VMEM((4, 32, 128), I32),
+            pltpu.VMEM((8, 128), F32),
+            pltpu.VMEM((4, 8, 128), F32),
         ]
         + [pltpu.VMEM((ROWS, 128), F32)] * 5
         + [
             dma,
-            dma((2,)),
+            dma((2, 2)),
             dma((6,)),
             dma((2, 6)),
             dma((8,)),
@@ -582,6 +645,8 @@
             dma((8,)),
             dma,
             dma,
+            dma((8,)),
+            dma((4,)),
         ],
         compiler_params=pltpu.CompilerParams(
             collective_id=0, has_side_effects=True, vmem_limit_bytes=50 * 1024 * 1024
@@ -589,7 +654,10 @@
     )(
         source.reshape(128, 256),
         storage.reshape(128, 256),
-        table,
+        host_device.reshape(1, 128),
+        host_column.reshape(1, 128),
+        inter_device.T,
+        inter_slot.T,
     )
     return result.reshape(source.shape)
 

time: 157 us -> 144 us (0.917)
  Pallas kernels: 153 us -> 140 us
    pallas_call x1, Pallas kernels: 153 us -> 140 us  [per_device(): pl.pallas_call(kernel, out_shape=jax.ShapeDtypeStruct((128, 256), F32), i...]
    unnamed x15 -> x13, local copies, waits for them, and re-layouts: 2.81 us -> 3.17 us
where the time goes in v3:
time: 144 us; the launch traced here: 143 us
  Pallas kernels  140 us (97%)
  local copies, waits for them, and re-layouts  3.17 us (2%)
    pallas_call x1, Pallas kernels, per_device(): pl.pallas_call(kernel, out_shape=jax.ShapeDtypeStruct((128, 256), F32), i...  140 us
    unnamed x13, local copies, waits for them, and re-layouts  3.17 us

profile of v3, /device:TPU:3, one launch (start us, length us, event | category | flops | bytes accessed | tf_op | source)
XLA Modules:
  0.0 143.4 jit_solution(7446280094009462906)
XLA Ops:
  0.0 0.0 copy-start.3
  0.0 0.0 copy-start.5
  0.0 0.0 copy-start.2
  0.0 0.0 copy-start.4
  0.0 0.7 copy-done.3
  0.7 0.0 copy-done.5
  0.7 0.0 copy-done.2
  0.7 0.0 copy-done.4
  0.7 0.0 copy-start
  0.7 0.9 copy-done
  1.6 0.0 copy-start.1
  1.6 0.9 copy-done.1
  2.5 140.2 %shard_map.64 = f32[128,256]{1,0:T(8,128)S(1)} custom-call(f32[128,256]{1,0:T(8,128)S(1)} %bitcast.8, f32[128,256]{1,0:T(8,128)S(1)} %bitcast.9, s32[1,128]{1,0:T(1,128)S(1)} %bitcast.12, s32[1,128]{1,0:T(1,128)S(1)} %bitcast.13, s32[2,128]{1,0:T(2,128)S(1)} %bitcast.10, s32[2,128]{1,0:T(2,128)S(1)} %bitcast.11), custom_call_target="tpu_custom_call" | custom-call | tf_op jit(solution)/shard_map/pallas_call | solution.py:605
  142.7 0.7 copy.8
Async XLA Ops:
  0.0 0.7 copy-start.3
  0.0 0.7 copy-start.5
  0.0 0.7 copy-start.2
  0.0 0.7 copy-start.4
  0.7 0.9 copy-start
  1.6 0.9 copy-start.1

commit v4 on v3

--- a/solution.py
+++ b/solution.py
@@ -65,7 +65,8 @@
         return ((w_ // 2) % 2, (w_ // 4) * 16 + z_ * 2 + w_ % 2, y_)
 
     def peer(k):
-        return place((w + k % 8) % 8, (gy + k // 8 + k % 8) % 4, cz)
+        n = (k + 1) % PEERS
+        return place((w + n % 8) % 8, (gy + n // 8 + n % 8) % 4, cz)
 
     w_home = gx // 4
     u_home = gx % 4
@@ -80,7 +81,7 @@
         greet(peer(k))
         return carry
 
-    lax.fori_loop(1, PEERS, greet_peer, 0)
+    lax.fori_loop(0, PEERS - 1, greet_peer, 0)
     greet(place(w, gy, (cz + 1) % 8))
     greet(place(w, gy, (cz + 7) % 8))
 
@@ -203,7 +204,8 @@
     k32 = lax.broadcasted_iota(I32, (32, 128), 0)
     table = er[...].reshape(32, 128)
     table = jnp.concatenate([table] * 4, axis=0)
-    first_of = ((w + k32 % 8) % 8) * 16 + (gy + k32 // 8 + k32 % 8) % 4
+    n32 = (k32 + 1) % PEERS
+    first_of = ((w + n32 % 8) % 8) * 16 + (gy + n32 // 8 + n32 % 8) % 4
     outgoing = jnp.zeros((32, 128), F32)
     for ub in range(4):
         chosen = jnp.where(first_of + ub * 4 == l32, 1.0, 0.0)
@@ -213,7 +215,7 @@
         )
         outgoing = jnp.where(ub1 == ub, x, outgoing)
     mo[...] = jnp.broadcast_to(outgoing[:, None, :], (32, 8, 128)).reshape(256, 128)
-    mi[0:8] = mo[0:8]
+    mi[248:256] = mo[248:256]
 
     def edge_send(k, carry):
         at = pl.multiple_of(k * 8, 8)
@@ -227,12 +229,50 @@
         ).start()
         return carry
 
-    lax.fori_loop(1, PEERS, edge_send, 0)
-
-    pltpu.make_async_copy(mi.at[pl.ds(8, 248)], mi.at[pl.ds(8, 248)], mrecv_sem).wait()
+    lax.fori_loop(0, PEERS - 1, edge_send, 0)
+
+    def far_wait(n, carry):
+        mine = own & (n == g * 4 + u_home)
+
+        @pl.when(jnp.logical_not(mine))
+        def _():
+            pltpu.make_async_copy(rx.at[n], rx.at[n], trecv_sem.at[n]).wait()
+
+        @pl.when(jnp.logical_not(own & (n == cz)))
+        def _():
+            pltpu.make_async_copy(tx.at[n], tx.at[n], tsend_sem.at[n]).wait()
+
+        return carry
+
+    lax.fori_loop(0, 8, far_wait, 0)
+
+    ln = lanes(ROWS)
+    group = ln // 32
+    is_f = ln < 32
+    is_m = group == 1
+
+    pairs, theta = coefficients()
+    for a, ref in ((0, r_ref), (1, c_ref)):
+        for u in range(4):
+            fr = rx[4 + u, a * 32:(a + 1) * 32, :]
+            ma = rx[u, a * 32:(a + 1) * 32, :]
+            for q in range(4):
+                ref[u * 128 + q * 32:u * 128 + (q + 1) * 32, :] = jnp.where(
+                    l32 < 32,
+                    turn(fr, -32 * q),
+                    jnp.where(l32 // 32 == 1, turn(ma, 32 - 32 * q), 0.0),
+                )
+    stored = c_ref[...]
+    inverse = 1.0 / (stored + jnp.where(is_f, 4.0 * TF + 4.0 * TI + TM, 6.0 + TM))
+    i_ref[...] = inverse
+    c_ref[...] = stored
+    d_ref[...] = r_ref[...] * inverse * (1.0 / theta)
+    p_ref[...] = jnp.zeros((ROWS, 128), F32)
+
+    pltpu.make_async_copy(mi.at[pl.ds(0, 248)], mi.at[pl.ds(0, 248)], mrecv_sem).wait()
     incoming = mi[pl.ds(0, 32, stride=8), :]
-    mirror_w = (8 - k32 % 8) % 8
-    mirror = mirror_w + 8 * ((16 - k32 // 8 - k32 % 8 - mirror_w) % 4)
+    mirror = (8 - n32 % 8) % 8
+    mirror = (mirror + 8 * ((16 - n32 // 8 - n32 % 8 - mirror) % 4) + PEERS - 1) % PEERS
     mirror = jnp.where(mirror == l32, 1.0, 0.0)[:, :32]
 
     def mirrored(x):
@@ -308,84 +348,6 @@
 
     lax.fori_loop(0, 16, build_g, 0)
 
-    across = (((1,), (1,)), ((), ()))
-    sbf = lax.dot_general(q_row, rf[...], across, preferred_element_type=F32).astype(I32)
-    sbm = lax.dot_general(q_row, rm[...], across, preferred_element_type=F32).astype(I32)
-    within = lax.broadcasted_iota(I32, (1, 1280), 1) % 40
-    weight = jnp.where(within < 32, TI, TM)
-
-    def build_s(j, carry):
-        at = pl.multiple_of(j * 16, 16)
-        block = lax.broadcasted_iota(I32, (16, 1280), 0) + (at + 1)
-        for q in range(4):
-            sf[pl.ds(at + q * ROWS, 16), :] = jnp.where(sbf[q:q + 1, :] == block, weight, 0.0).astype(BF16)
-            sm[pl.ds(at + q * ROWS, 16), :] = jnp.where(
-                sbm[q:q + 1, :] == block[:, :256], TM, 0.0
-            ).astype(BF16)
-        return carry
-
-    lax.fori_loop(0, 32, build_s, 0)
-
-    def far_wait(n, carry):
-        mine = own & (n == g * 4 + u_home)
-
-        @pl.when(jnp.logical_not(mine))
-        def _():
-            pltpu.make_async_copy(rx.at[n], rx.at[n], trecv_sem.at[n]).wait()
-
-        @pl.when(jnp.logical_not(own & (n == cz)))
-        def _():
-            pltpu.make_async_copy(tx.at[n], tx.at[n], tsend_sem.at[n]).wait()
-
-        return carry
-
-    lax.fori_loop(0, 8, far_wait, 0)
-
-    ln = lanes(ROWS)
-    group = ln // 32
-    is_f = ln < 32
-    is_m = group == 1
-
-    pairs, theta = coefficients()
-    for a, ref in ((0, r_ref), (1, c_ref)):
-        for u in range(4):
-            fr = rx[4 + u, a * 32:(a + 1) * 32, :]
-            ma = rx[u, a * 32:(a + 1) * 32, :]
-            for q in range(4):
-                ref[u * 128 + q * 32:u * 128 + (q + 1) * 32, :] = jnp.where(
-                    l32 < 32,
-                    turn(fr, -32 * q),
-                    jnp.where(l32 // 32 == 1, turn(ma, 32 - 32 * q), 0.0),
-                )
-    stored = c_ref[...]
-    inverse = 1.0 / (stored + jnp.where(is_f, 4.0 * TF + 4.0 * TI + TM, 6.0 + TM))
-    i_ref[...] = inverse
-    c_ref[...] = stored
-    d_ref[...] = r_ref[...] * inverse * (1.0 / theta)
-    p_ref[...] = jnp.zeros((ROWS, 128), F32)
-
-    entering = jnp.where(lax.broadcasted_iota(I32, (1280, 128), 0) % 40 < 16, 1.0, 0.0).astype(BF16)
-    ones = jnp.ones((256, 128), BF16)
-    indeg = jnp.zeros((ROWS, 128), F32)
-    hosted = jnp.zeros((ROWS, 128), F32)
-    for q in range(4):
-        indeg = indeg + jnp.dot(sf[q * ROWS:(q + 1) * ROWS, :], entering, preferred_element_type=F32)
-        hosted = hosted + jnp.dot(sm[q * ROWS:(q + 1) * ROWS, :], ones, preferred_element_type=F32)
-
-    c_ref[...] = c_ref[...] + jnp.where(is_f, 4.0 * TF + 2.0 * TI + TM + indeg, 6.0 + hosted)
-    pltpu.make_async_copy(mo.at[pl.ds(8, 248)], mo.at[pl.ds(8, 248)], msend_sem).wait()
-
-    def edge_sent(z, carry):
-        @pl.when(jnp.logical_not(own & (z == cz)))
-        def _():
-            pltpu.make_async_copy(et, et, esend_sem.at[z]).wait()
-
-        return carry
-
-    @pl.when(g == 0)
-    def _():
-        lax.fori_loop(0, 8, edge_sent, 0)
-
     low = jnp.where(cz > 0, 1.0, 0.0)
     high = jnp.where(cz < 7, 1.0, 0.0)
     left = jnp.where(w > 0, 1.0, 0.0)
@@ -401,8 +363,7 @@
     def unpacked(x):
         return jnp.concatenate([turn(x, -32 * q) for q in range(4)], axis=0)
 
-    def step(t, carry):
-        par = t % 2
+    def halo_copies(par):
 
         def halo(n, source, dest, device):
             return pltpu.make_async_remote_copy(
@@ -414,7 +375,7 @@
                 device_id_type=MESH,
             )
 
-        halos = [
+        return [
             halo(0, hs.at[0], hz.at[par, 0], place(w, gy, (cz + 1) % 8)),
             halo(1, hs.at[1], hz.at[par, 1], place(w, gy, (cz + 7) % 8)),
             halo(2, ys.at[1], hy.at[par, 0], place(w, (gy + 1) % 4, cz)),
@@ -422,6 +383,9 @@
             halo(4, d_ref.at[pl.ds(ROWS - 8, 8)], hx.at[par, 0], place((w + 1) % 8, gy, cz)),
             halo(5, d_ref.at[pl.ds(0, 8)], hx.at[par, 1], place((w + 7) % 8, gy, cz)),
         ]
+    def launch(t):
+        par = t % 2
+        halos = halo_copies(par)
         d = d_ref[...]
         high_part = d.astype(BF16).astype(F32)
         low_part = d - high_part
@@ -454,8 +418,12 @@
             send[pl.ds(c * 8, 8), 40:48, :] = (x[:, :128] + x[:, 128:]).reshape(8, 8, 128)
             for n in range(8):
                 k = c * 8 + n
-                if n > 0 or not isinstance(c, int):
+                if n < 7 or isinstance(c, int):
                     message(k, c // 2).start()
+                else:
+                    @pl.when(c < 3)
+                    def _():
+                        message(k, c // 2).start()
             return carry
 
         gather(0, 0)
@@ -466,8 +434,12 @@
         for copy in halos:
             copy.start()
         lax.fori_loop(1, 4, gather, 0)
-        recv[par, 0] = send[0]
-
+        recv[par, PEERS - 1] = send[PEERS - 1]
+
+    def finish(t):
+        par = t % 2
+        halos = halo_copies(par)
+        d = d_ref[...]
         col = ln % 16
         before = turn(d, 1)
         after = turn(d, -1)
@@ -499,7 +471,7 @@
         sum_f = jnp.zeros((ROWS, 128), F32)
         sum_m = jnp.zeros((ROWS, 128), F32)
         for half in range(2):
-            came = recv.at[par, pl.ds(1, 15)] if half == 0 else recv.at[par, pl.ds(16, 16)]
+            came = recv.at[par, pl.ds(0, 16)] if half == 0 else recv.at[par, pl.ds(16, 15)]
             pltpu.make_async_copy(came, came, recv_sem.at[par, half]).wait()
             x = recv[par, half * 16:(half + 1) * 16, 8:48, :].reshape(640, 128)
             hi = x.astype(BF16)
@@ -535,7 +507,7 @@
         for copy in halos:
             copy.wait_send()
         pltpu.make_async_copy(
-            send.at[pl.ds(1, PEERS - 1)], send.at[pl.ds(1, PEERS - 1)], send_sem
+            send.at[pl.ds(0, PEERS - 1)], send.at[pl.ds(0, PEERS - 1)], send_sem
         ).wait()
         phase = t % 4
         alpha = jnp.float32(pairs[3][0])
@@ -546,6 +518,56 @@
         r = r_ref[...] + total
         r_ref[...] = r
         d_ref[...] = alpha * d_ref[...] + beta * (r * i_ref[...])
+
+    launch(0)
+
+    across = (((1,), (1,)), ((), ()))
+    sbf = lax.dot_general(q_row, rf[...], across, preferred_element_type=F32).astype(I32)
+    sbm = lax.dot_general(q_row, rm[...], across, preferred_element_type=F32).astype(I32)
+    within = lax.broadcasted_iota(I32, (1, 1280), 1) % 40
+    weight = jnp.where(within < 32, TI, TM)
+
+    def build_s(j, carry):
+        at = pl.multiple_of(j * 16, 16)
+        block = lax.broadcasted_iota(I32, (16, 1280), 0) + (at + 1)
+        for q in range(4):
+            sf[pl.ds(at + q * ROWS, 16), :] = jnp.where(sbf[q:q + 1, :] == block, weight, 0.0).astype(BF16)
+            sm[pl.ds(at + q * ROWS, 16), :] = jnp.where(
+                sbm[q:q + 1, :] == block[:, :256], TM, 0.0
+            ).astype(BF16)
+        return carry
+
+    lax.fori_loop(0, 32, build_s, 0)
+
+    entering = jnp.where(lax.broadcasted_iota(I32, (1280, 128), 0) % 40 < 16, 1.0, 0.0).astype(BF16)
+    ones = jnp.ones((256, 128), BF16)
+    indeg = jnp.zeros((ROWS, 128), F32)
+    hosted = jnp.zeros((ROWS, 128), F32)
+    for q in range(4):
+        indeg = indeg + jnp.dot(sf[q * ROWS:(q + 1) * ROWS, :], entering, preferred_element_type=F32)
+        hosted = hosted + jnp.dot(sm[q * ROWS:(q + 1) * ROWS, :], ones, preferred_element_type=F32)
+
+    c_ref[...] = c_ref[...] + jnp.where(is_f, 4.0 * TF + 2.0 * TI + TM + indeg, 6.0 + hosted)
+    pltpu.make_async_copy(mo.at[pl.ds(0, 248)], mo.at[pl.ds(0, 248)], msend_sem).wait()
+
+    def edge_sent(z, carry):
+        @pl.when(jnp.logical_not(own & (z == cz)))
+        def _():
+            pltpu.make_async_copy(et, et, esend_sem.at[z]).wait()
+
+        return carry
+
+    @pl.when(g == 0)
+    def _():
+        lax.fori_loop(0, 8, edge_sent, 0)
+
+    def step(t, carry):
+        finish(t)
+
+        @pl.when(t < STEPS - 1)
+        def _():
+            launch(t + 1)
+
         return carry
 
     lax.fori_loop(0, STEPS, step, 0)

time: 144 us -> 141 us (0.979)
  Pallas kernels: 140 us -> 138 us
    pallas_call x1, Pallas kernels: 140 us -> 138 us  [per_device(): pl.pallas_call(kernel, out_shape=jax.ShapeDtypeStruct((128, 256), F32), i...]
where the time goes in v4:
time: 141 us
  Pallas kernels  138 us (98%)
  local copies, waits for them, and re-layouts  3.17 us (2%)
    pallas_call x1, Pallas kernels, per_device(): pl.pallas_call(kernel, out_shape=jax.ShapeDtypeStruct((128, 256), F32), i...  138 us
    unnamed x13, local copies, waits for them, and re-layouts  3.17 us

profile of v4, /device:TPU:3, one launch (start us, length us, event | category | flops | bytes accessed | tf_op | source)
XLA Modules:
  0.0 140.7 jit_solution(10082165480711353868)
XLA Ops:
  0.0 0.0 copy-start.3
  0.0 0.0 copy-start.5
  0.0 0.0 copy-start.2
  0.0 0.0 copy-start.4
  0.0 0.7 copy-done.3
  0.7 0.0 copy-done.5
  0.7 0.0 copy-done.2
  0.7 0.0 copy-done.4
  0.7 0.0 copy-start
  0.7 0.9 copy-done
  1.6 0.0 copy-start.1
  1.6 0.9 copy-done.1
  2.5 137.5 %shard_map.64 = f32[128,256]{1,0:T(8,128)S(1)} custom-call(f32[128,256]{1,0:T(8,128)S(1)} %bitcast.8, f32[128,256]{1,0:T(8,128)S(1)} %bitcast.9, s32[1,128]{1,0:T(1,128)S(1)} %bitcast.12, s32[1,128]{1,0:T(1,128)S(1)} %bitcast.13, s32[2,128]{1,0:T(2,128)S(1)} %bitcast.10, s32[2,128]{1,0:T(2,128)S(1)} %bitcast.11), custom_call_target="tpu_custom_call" | custom-call | tf_op jit(solution)/shard_map/pallas_call | solution.py:627
  140.0 0.7 copy.8
Async XLA Ops:
  0.0 0.7 copy-start.3
  0.0 0.7 copy-start.5
  0.0 0.7 copy-start.2
  0.0 0.7 copy-start.4
  0.7 0.9 copy-start
  1.6 0.9 copy-start.1

commit v5 on v4

--- a/solution.py
+++ b/solution.py
@@ -65,7 +65,7 @@
         return ((w_ // 2) % 2, (w_ // 4) * 16 + z_ * 2 + w_ % 2, y_)
 
     def peer(k):
-        n = (k + 1) % PEERS
+        n = 31 - k
         return place((w + n % 8) % 8, (gy + n // 8 + n % 8) % 4, cz)
 
     w_home = gx // 4
@@ -81,22 +81,22 @@
         greet(peer(k))
         return carry
 
+
+    def greet_far(n, carry):
+        @pl.when(jnp.logical_not(own & (n == cz)))
+        def _():
+            greet(place(w_home, gy, n))
+
+        @pl.when(jnp.logical_not(own & (n == g * 4 + u_home)))
+        def _():
+            greet((n // 4, w * 4 + n % 4, gy))
+
+        return carry
+
+    lax.fori_loop(0, 8, greet_far, 0)
     lax.fori_loop(0, PEERS - 1, greet_peer, 0)
     greet(place(w, gy, (cz + 1) % 8))
     greet(place(w, gy, (cz + 7) % 8))
-
-    def greet_far(n, carry):
-        @pl.when(jnp.logical_not(own & (n == cz)))
-        def _():
-            greet(place(w_home, gy, n))
-
-        @pl.when(jnp.logical_not(own & (n == g * 4 + u_home)))
-        def _():
-            greet((n // 4, w * 4 + n % 4, gy))
-
-        return carry
-
-    lax.fori_loop(0, 8, greet_far, 0)
 
     l128 = lanes(128)
     s128 = lax.broadcasted_iota(I32, (128, 128), 0)
@@ -204,7 +204,7 @@
     k32 = lax.broadcasted_iota(I32, (32, 128), 0)
     table = er[...].reshape(32, 128)
     table = jnp.concatenate([table] * 4, axis=0)
-    n32 = (k32 + 1) % PEERS
+    n32 = 31 - k32
     first_of = ((w + n32 % 8) % 8) * 16 + (gy + n32 // 8 + n32 % 8) % 4
     outgoing = jnp.zeros((32, 128), F32)
     for ub in range(4):
@@ -272,7 +272,7 @@
     pltpu.make_async_copy(mi.at[pl.ds(0, 248)], mi.at[pl.ds(0, 248)], mrecv_sem).wait()
     incoming = mi[pl.ds(0, 32, stride=8), :]
     mirror = (8 - n32 % 8) % 8
-    mirror = (mirror + 8 * ((16 - n32 // 8 - n32 % 8 - mirror) % 4) + PEERS - 1) % PEERS
+    mirror = 31 - (mirror + 8 * ((16 - n32 // 8 - n32 % 8 - mirror) % 4))
     mirror = jnp.where(mirror == l32, 1.0, 0.0)[:, :32]
 
     def mirrored(x):

time: 141 us -> 140 us (level)
  no operation moved by 1% of the time
where the time goes in v5:
time: 140 us
  Pallas kernels  137 us (98%)
  local copies, waits for them, and re-layouts  3.17 us (2%)
    pallas_call x1, Pallas kernels, per_device(): pl.pallas_call(kernel, out_shape=jax.ShapeDtypeStruct((128, 256), F32), i...  137 us
    unnamed x13, local copies, waits for them, and re-layouts  3.17 us

profile of v5, /device:TPU:3, one launch (start us, length us, event | category | flops | bytes accessed | tf_op | source)
XLA Modules:
  0.0 139.8 jit_solution(15841050243842976155)
XLA Ops:
  0.0 0.0 copy-start.3
  0.0 0.0 copy-start.5
  0.0 0.0 copy-start.2
  0.0 0.0 copy-start.4
  0.0 0.7 copy-done.3
  0.7 0.0 copy-done.5
  0.7 0.0 copy-done.2
  0.7 0.0 copy-done.4
  0.7 0.0 copy-start
  0.7 0.9 copy-done
  1.6 0.0 copy-start.1
  1.6 0.9 copy-done.1
  2.5 136.6 %shard_map.64 = f32[128,256]{1,0:T(8,128)S(1)} custom-call(f32[128,256]{1,0:T(8,128)S(1)} %bitcast.8, f32[128,256]{1,0:T(8,128)S(1)} %bitcast.9, s32[1,128]{1,0:T(1,128)S(1)} %bitcast.12, s32[1,128]{1,0:T(1,128)S(1)} %bitcast.13, s32[2,128]{1,0:T(2,128)S(1)} %bitcast.10, s32[2,128]{1,0:T(2,128)S(1)} %bitcast.11), custom_call_target="tpu_custom_call" | custom-call | tf_op jit(solution)/shard_map/pallas_call | solution.py:627
  139.2 0.7 copy.8
Async XLA Ops:
  0.0 0.7 copy-start.3
  0.0 0.7 copy-start.5
  0.0 0.7 copy-start.2
  0.0 0.7 copy-start.4
  0.7 0.9 copy-start
  1.6 0.9 copy-start.1

commit v6 on v5

--- a/solution.py
+++ b/solution.py
@@ -269,8 +269,6 @@
     d_ref[...] = r_ref[...] * inverse * (1.0 / theta)
     p_ref[...] = jnp.zeros((ROWS, 128), F32)
 
-    pltpu.make_async_copy(mi.at[pl.ds(0, 248)], mi.at[pl.ds(0, 248)], mrecv_sem).wait()
-    incoming = mi[pl.ds(0, 32, stride=8), :]
     mirror = (8 - n32 % 8) % 8
     mirror = 31 - (mirror + 8 * ((16 - n32 // 8 - n32 % 8 - mirror) % 4))
     mirror = jnp.where(mirror == l32, 1.0, 0.0)[:, :32]
@@ -287,8 +285,6 @@
         return jnp.where(x > 0, ub1 * 128 + ((x - 1) & 127) + 1, 0)
 
     vs[0] = source_row(outgoing)
-    vs[1] = target_row(mirrored(incoming))
-    vs[2] = target_row(incoming)
     vs[3] = source_row(mirrored(outgoing))
 
     inter_at = jnp.where(t1 < 4, ua1 * 4 + ub1, -100)
@@ -316,6 +312,11 @@
 
     def halves(x):
         return jnp.concatenate([(x >> 5).astype(F32), (x & 31).astype(F32)], axis=1).astype(BF16)
+
+    pltpu.make_async_copy(mi.at[pl.ds(0, 248)], mi.at[pl.ds(0, 248)], mrecv_sem).wait()
+    incoming = mi[pl.ds(0, 32, stride=8), :]
+    vs[1] = target_row(mirrored(incoming))
+    vs[2] = target_row(incoming)
 
     def build_g(j, carry):
         def pair(n, first):

time: 140 us -> 140 us (level)
  no operation moved by 1% of the time
where the time goes in v6:
time: 140 us
  Pallas kernels  137 us (98%)
  local copies, waits for them, and re-layouts  3.17 us (2%)
    pallas_call x1, Pallas kernels, per_device(): pl.pallas_call(kernel, out_shape=jax.ShapeDtypeStruct((128, 256), F32), i...  137 us
    unnamed x13, local copies, waits for them, and re-layouts  3.17 us

profile of v6, /device:TPU:3, one launch (start us, length us, event | category | flops | bytes accessed | tf_op | source)
XLA Modules:
  0.0 140.0 jit_solution(15351855192199440190)
XLA Ops:
  0.0 0.0 copy-start.3
  0.0 0.0 copy-start.5
  0.0 0.0 copy-start.2
  0.0 0.0 copy-start.4
  0.0 0.7 copy-done.3
  0.7 0.0 copy-done.5
  0.7 0.0 copy-done.2
  0.7 0.0 copy-done.4
  0.7 0.0 copy-start
  0.7 0.9 copy-done
  1.6 0.0 copy-start.1
  1.6 0.9 copy-done.1
  2.5 136.8 %shard_map.64 = f32[128,256]{1,0:T(8,128)S(1)} custom-call(f32[128,256]{1,0:T(8,128)S(1)} %bitcast.8, f32[128,256]{1,0:T(8,128)S(1)} %bitcast.9, s32[1,128]{1,0:T(1,128)S(1)} %bitcast.12, s32[1,128]{1,0:T(1,128)S(1)} %bitcast.13, s32[2,128]{1,0:T(2,128)S(1)} %bitcast.10, s32[2,128]{1,0:T(2,128)S(1)} %bitcast.11), custom_call_target="tpu_custom_call" | custom-call | tf_op jit(solution)/shard_map/pallas_call | solution.py:628
  139.3 0.7 copy.8
Async XLA Ops:
  0.0 0.7 copy-start.3
  0.0 0.7 copy-start.5
  0.0 0.7 copy-start.2
  0.0 0.7 copy-start.4
  0.7 0.9 copy-start
  1.6 0.9 copy-start.1

commit v7 on v6

--- a/solution.py
+++ b/solution.py
@@ -428,13 +428,15 @@
             return carry
 
         gather(0, 0)
+        ys[0] = d_ref[pl.ds(0, 64, stride=8), :]
+        ys[1] = d_ref[pl.ds(7, 64, stride=8), :]
+        for copy in halos[2:]:
+            copy.start()
+        lax.fori_loop(1, 4, gather, 0)
         hs[0] = packed(jnp.where(ln < 16, turn(d, -16), turn(d, -47)))
         hs[1] = packed(jnp.where(ln < 16, d, turn(d, -16)))
-        ys[0] = d_ref[pl.ds(0, 64, stride=8), :]
-        ys[1] = d_ref[pl.ds(7, 64, stride=8), :]
-        for copy in halos:
+        for copy in halos[:2]:
             copy.start()
-        lax.fori_loop(1, 4, gather, 0)
         recv[par, PEERS - 1] = send[PEERS - 1]
 
     def finish(t):

time: 140 us -> 140 us (level)
  no operation moved by 1% of the time
where the time goes in v7:
time: 140 us; the launch traced here: 139 us
  Pallas kernels  136 us (97%)
  local copies, waits for them, and re-layouts  3.17 us (2%)
    pallas_call x1, Pallas kernels, per_device(): pl.pallas_call(kernel, out_shape=jax.ShapeDtypeStruct((128, 256), F32), i...  136 us
    unnamed x13, local copies, waits for them, and re-layouts  3.17 us

profile of v7, /device:TPU:3, one launch (start us, length us, event | category | flops | bytes accessed | tf_op | source)
XLA Modules:
  0.0 139.4 jit_solution(5858326917066350810)
XLA Ops:
  0.0 0.0 copy-start.3
  0.0 0.0 copy-start.5
  0.0 0.0 copy-start.2
  0.0 0.0 copy-start.4
  0.0 0.7 copy-done.3
  0.7 0.0 copy-done.5
  0.7 0.0 copy-done.2
  0.7 0.0 copy-done.4
  0.7 0.0 copy-start
  0.7 0.9 copy-done
  1.6 0.0 copy-start.1
  1.6 0.9 copy-done.1
  2.5 136.2 %shard_map.64 = f32[128,256]{1,0:T(8,128)S(1)} custom-call(f32[128,256]{1,0:T(8,128)S(1)} %bitcast.8, f32[128,256]{1,0:T(8,128)S(1)} %bitcast.9, s32[1,128]{1,0:T(1,128)S(1)} %bitcast.12, s32[1,128]{1,0:T(1,128)S(1)} %bitcast.13, s32[2,128]{1,0:T(2,128)S(1)} %bitcast.10, s32[2,128]{1,0:T(2,128)S(1)} %bitcast.11), custom_call_target="tpu_custom_call" | custom-call | tf_op jit(solution)/shard_map/pallas_call | solution.py:630
  138.7 0.7 copy.8
Async XLA Ops:
  0.0 0.7 copy-start.3
  0.0 0.7 copy-start.5
  0.0 0.7 copy-start.2
  0.0 0.7 copy-start.4
  0.7 0.9 copy-start
  1.6 0.9 copy-start.1
